TPU v7x, 128 devices: a whole 4x4x4 slice. The times are simulated.
128 devices in a mesh: group: 8 (over y, core), seq: 16 (over z, x).
Axes of the slice: x: 4, y: 4, z: 4, core: 2. Of those that a mesh axis runs over, the one named last changes fastest.
Arguments:
- q_nope: bfloat16 [32, 3, 128, 128], P('group', None, 'seq'), may hold values from -6 to 6
- q_rope: bfloat16 [32, 3, 128, 64], P('group', None, 'seq'), may hold values from -7 to 7
- w_absorb: bfloat16 [128, 128, 512], P('seq'), may hold values from -0.5 to 0.5
- w_value: bfloat16 [128, 512, 128], P('seq'), may hold values from -0.25 to 0.25
- cache: bfloat16 [16, 32768, 576], P('group', 'seq'), may hold values from -7 to 7
- res_len: int32 [16], P('group'), may hold values from 4096 to 32768
- prefill_rows: bfloat16 [8, 128, 128, 576], P('group', 'seq'), may hold values from -7 to 7
- block_dest: int32 [8, 128], P('group', 'seq'), may hold values from 0 to 15, as said below
- new_rows: bfloat16 [32, 3, 576], P('group'), may hold values from -7 to 7
Outputs:
- attention_out: bfloat16 [32, 3, 128, 128], P('group', None, 'seq')
Inputs may be any that keep to these rules, and one draw needn't show every extreme that they name: `block_dest`: each prefill device sends at most 2 blocks to any one decode group (value // 2); for every index along seq one decode group gets exactly 2 blocks from the device of that index in every group, at least one for each of its new requests.
All inputs are finite; a program needn't handle non-finite values.
Results may differ from a plain program's by a relative error of at most 0.0081.
Values may be sent and summed in bfloat16 or wider, within the bound.
A program may use at most 192 MiB of HBM per device.

v0:
```python
import jax
import jax.numpy as jnp
from jax import lax
from jax.sharding import PartitionSpec as P

RES = 2
NEWD = 2
CAP = 2


masked_score = -1e30


def merged(part, axis, combine):
    gathered = jax.tree.map(lambda a: lax.all_gather(a, axis), part)

    def take(source):
        return jax.tree.map(lambda a: lax.dynamic_index_in_dim(a, source, 0, False), gathered)

    return lax.fori_loop(
        1, lax.axis_size(axis), lambda source, state: combine(state, take(source)), take(0)
    )


def partial_softmax(scores, usable):
    scores = jnp.where(usable, scores, masked_score)
    peaks = jnp.max(scores, axis=-1)
    weights = jnp.where(usable, jnp.exp(scores - peaks[..., None]), 0.0)
    return (peaks, jnp.sum(weights, axis=-1), weights.astype(jnp.bfloat16))


def combine_two(first, second):
    peak_first, total_first, weighted_first = first
    peak_second, total_second, weighted_second = second
    peaks = jnp.maximum(peak_first, peak_second)
    keep_first = jnp.exp(peak_first - peaks)
    keep_second = jnp.exp(peak_second - peaks)
    totals = total_first * keep_first + total_second * keep_second
    weighted = weighted_first * keep_first[..., None] + weighted_second * keep_second[..., None]
    return (peaks, totals, weighted)


def body(q_nope, q_rope, w_absorb, w_value, cache, res_len, prefill_rows, block_dest, new_rows):
    batch_size, step_count, heads_here, nope_width = q_nope.shape
    latent_width = w_absorb.shape[2]
    row_width = cache.shape[2]
    scaling = (nope_width + q_rope.shape[3]) ** (-0.5)
    q_latent = jnp.einsum(
        "bthn,hnl->bthl", q_nope, w_absorb, preferred_element_type=jnp.float32
    ).astype(jnp.bfloat16)
    own_query = jnp.concatenate([q_latent, q_rope], axis=-1)
    full_query = lax.all_gather(own_query, "seq", axis=2, tiled=True)
    heads_all = full_query.shape[2]
    flat_query = full_query.reshape(batch_size, step_count * heads_all, row_width)
    groups = lax.axis_size("group")
    nblocks = prefill_rows.shape[1]
    block_rows = prefill_rows.shape[2]
    local_rows = prefill_rows[0].reshape(nblocks, block_rows * row_width)
    owners = block_dest[0]
    target = owners // NEWD
    member = owners % NEWD
    match_group = (target[:, None] == jnp.arange(groups, dtype=jnp.int32)[None, :]).astype(
        jnp.int32
    )
    earlier = jnp.cumsum(match_group, axis=0) - match_group
    order_rank = jnp.sum(earlier * match_group, axis=1)
    slot_index = target * CAP + order_rank
    placed = slot_index[None, :] == jnp.arange(groups * CAP, dtype=jnp.int32)[:, None]
    send_rows = jnp.dot(
        placed.astype(jnp.bfloat16), local_rows, preferred_element_type=jnp.float32
    ).astype(jnp.bfloat16)
    send_rows = send_rows.reshape(groups * CAP, block_rows, row_width)
    send_tags = (jnp.sum(jnp.where(placed, member[None, :] + 1, 0), axis=1) - 1).astype(
        jnp.bfloat16
    )
    ctx_here = cache.shape[1]
    positions = lax.axis_index("seq") * ctx_here + jnp.arange(ctx_here, dtype=jnp.int32)
    usable_res = positions[None, None, :] < res_len[:, None, None]
    scores_res = (
        jnp.einsum("rmk,rnk->rmn", flat_query[:RES], cache, preferred_element_type=jnp.float32)
        * scaling
    )
    peak_res, total_res, weights_res = partial_softmax(scores_res, usable_res)
    weighted_res = jnp.einsum(
        "rmn,rnl->rml", weights_res, cache[:, :, :latent_width], preferred_element_type=jnp.float32
    )
    got_rows, got_tags = (
        lax.all_to_all(send_rows, "group", split_axis=0, concat_axis=0, tiled=True),
        lax.all_to_all(send_tags, "group", split_axis=0, concat_axis=0, tiled=True),
    )
    key_rows = got_rows.reshape(-1, row_width)
    row_tags = jnp.repeat(got_tags, block_rows)
    usable_new = (
        row_tags[None, None, :]
        == jnp.arange(NEWD, dtype=jnp.int32).astype(jnp.bfloat16)[:, None, None]
    )
    scores_new = (
        jnp.einsum("rmk,nk->rmn", flat_query[RES:], key_rows, preferred_element_type=jnp.float32)
        * scaling
    )
    peak_new, total_new, weights_new = partial_softmax(scores_new, usable_new)
    weighted_new = jnp.einsum(
        "rmn,nl->rml", weights_new, key_rows[:, :latent_width], preferred_element_type=jnp.float32
    )
    peaks = jnp.concatenate([peak_res, peak_new], axis=0).reshape(batch_size, step_count, heads_all)
    totals = jnp.concatenate([total_res, total_new], axis=0).reshape(
        batch_size, step_count, heads_all
    )
    weighted = jnp.concatenate([weighted_res, weighted_new], axis=0).reshape(
        batch_size, step_count, heads_all, latent_width
    )
    peaks, totals, weighted = merged((peaks, totals, weighted), "seq", combine_two)
    head_start = lax.axis_index("seq") * heads_here
    peaks = lax.dynamic_slice_in_dim(peaks, head_start, heads_here, 2)
    totals = lax.dynamic_slice_in_dim(totals, head_start, heads_here, 2)
    weighted = lax.dynamic_slice_in_dim(weighted, head_start, heads_here, 2)
    causal = jnp.arange(step_count)[:, None] >= jnp.arange(step_count)[None, :]
    scores_fresh = (
        jnp.einsum("bthk,bsk->bths", own_query, new_rows, preferred_element_type=jnp.float32)
        * scaling
    )
    peak_fresh, total_fresh, weights_fresh = partial_softmax(scores_fresh, causal[None, :, None, :])
    weighted_fresh = jnp.einsum(
        "bths,bsl->bthl",
        weights_fresh,
        new_rows[:, :, :latent_width],
        preferred_element_type=jnp.float32,
    )
    peaks, totals, weighted = combine_two(
        (peaks, totals, weighted), (peak_fresh, total_fresh, weighted_fresh)
    )
    attended = (weighted / totals[..., None]).astype(jnp.bfloat16)
    return jnp.einsum(
        "bthl,hlv->bthv", attended, w_value, preferred_element_type=jnp.float32
    ).astype(jnp.bfloat16)


def solution(mesh):
    in_specs = (
        P("group", None, "seq", None),
        P("group", None, "seq", None),
        P("seq", None, None),
        P("seq", None, None),
        P("group", "seq", None),
        P("group"),
        P("group", "seq", None, None),
        P("group", "seq"),
        P("group", None, None),
    )
    out_specs = P("group", None, "seq", None)
    return jax.shard_map(body, mesh=mesh, in_specs=in_specs, out_specs=out_specs, check_vma=False)
```

profile of v0, /device:TPU:0, one launch (start us, length us, event | category | flops | bytes accessed | tf_op | source)
XLA Modules:
  0.0 466.5 jit_solution(2603448673843429078)
XLA Ops:
  11.9 4.6 all-to-all-start
  20.0 2.2 convolution_convert_fusion
  22.2 4.4 reshape.146
  26.6 2.6 copy.65
  29.2 4.8 %all-to-all-start.1 = ((bf16[16,128,576]{1,2,0:T(8,128)(2,1)}), bf16[16,128,576]{1,2,0:T(8,128)(2,1)S(1)}, u32[]{:S(2)}, u32[]{:S(2)}) async-start(bf16[16,128,576]{1,2,0:T(8,128)(2,1)} %copy.65), calls=%async_computation.1 | async-start | bytes 4718592 | tf_op jit(solution)/shard_map/all_to_all | solution.py:88
  34.6 29.4 %all-to-all-done.1 = bf16[16,128,576]{1,2,0:T(8,128)(2,1)S(1)} async-done(((bf16[16,128,576]{1,2,0:T(8,128)(2,1)}), bf16[16,128,576]{1,2,0:T(8,128)(2,1)S(1)}, u32[]{:S(2)}, u32[]{:S(2)}) %all-to-all-start.1) | async-done | bytes 2359328 | tf_op jit(solution)/shard_map/all_to_all | solution.py:88
  64.0 2.9 copy.66
  66.9 4.9 %reshape.149 = bf16[2048,576,1]{0,1,2:T(8,128)(2,1)} reshape(bf16[16,128,576]{1,0,2:T(8,128)(2,1)} %copy.66) | data formatting | bytes 4718592 | tf_op jit(solution)/shard_map/reshape | solution.py:91
  73.6 3.9 fusion.63
  77.8 5.1 %fusion.6 = (f32[2,384]{1,0:T(2,128)S(1)}, f32[2,384,2048]{2,1,0:T(8,128)S(1)}) fusion(pred[2,2048]{1,0:T(4,128)(4,1)S(1)} %broadcast_compare_fusion, bf16[2,384,576]{2,1,0:T(8,128)(2,1)S(1)} %bitcast.94, bf16[2,2048,576]{1,2,0:T(8,128)(2,1)} %param.15), kind=kOutput, calls=%fused_computation.17 | convolution fusion | flops 1816657152 | bytes 11901952 | tf_op jit(solution)/shard_map/rmk,rnk->rmn/dot_general | solution.py:80
  86.4 2.9 fusion.7
  94.5 6.3 %fusion.9 = (f32[2,384]{1,0:T(2,128)S(1)}, f32[2,384]{1,0:T(2,128)S(1)}) fusion(f32[2,384,2048]{2,1,0:T(8,128)} %copy-done.2, f32[2,384]{1,0:T(2,128)S(1)} %get-tuple-element.236, pred[2,2048]{1,0:T(4,128)(4,1)S(1)} %broadcast_compare_fusion, f32[2,384]{1,0:T(2,128)S(1)} %get-tuple-element.234, f32[2,384,2048]{2,1,0:T(8,128)} %copy-done.3, ...), kind=kLoop, calls=%fused_computation.20 | loop fusion | flops 15727104 | bytes 12603392 | tf_op jit(solution)/shard_map/reduce_sum | solution.py:29
  100.8 25.2 %all_gather.14 = f32[16,4,3,128]{3,1,2,0:T(4,128)S(1)} all-gather(f32[1,4,3,128]{3,1,2,0:T(4,128)S(1)} %maximum_bitcast_fusion.1), channel_id=1, replica_groups=mesh['group'=8,'seq'=16] {'seq'}, dimensions={0}, use_global_device_ids=true | all-gather | bytes 104448 | tf_op jit(solution)/shard_map/all_gather | solution.py:15
  126.0 23.1 %all_gather.13 = f32[16,4,3,128]{3,1,2,0:T(4,128)S(1)} all-gather(f32[1,4,3,128]{3,1,2,0:T(4,128)S(1)} %maximum_bitcast_fusion), channel_id=1, replica_groups=mesh['group'=8,'seq'=16] {'seq'}, dimensions={0}, use_global_device_ids=true | all-gather | bytes 104448 | tf_op jit(solution)/shard_map/all_gather | solution.py:15
  149.2 229.2 %all-gather.5.cloned.1.call-done = f32[16,4,3,128,512]{4,3,2,1,0:T(8,128)} async-done(((f32[1,4,3,128,512]{4,3,2,1,0:T(8,128)}), f32[16,4,3,128,512]{4,3,2,1,0:T(8,128)}) %all-gather.5.cloned.1.call-update) | async-done | bytes 50331664 | tf_op jit(solution)/shard_map/all_gather | solution.py:15
  378.4 3.8 slice_bitcast_fusion
  382.2 75.2 %while.19 = (s32[]{:T(128)}, f32[4,3,128]{2,1,0:T(4,128)S(1)}, f32[4,3,128]{2,1,0:T(4,128)S(1)}, f32[4,3,128,512]{3,2,1,0:T(8,128)}, f32[16,4,3,128]{3,1,2,0:T(4...) while((s32[]{:T(128)}, f32[4,3,128]{2,1,0:T(4,128)S(1)}, ...), condition=%wide.region_8.9_spmd, body=%wide.region_7.8_spmd.sunk | while | flops 2368517 | bytes 9523343 | solution.py:20
  382.2 5.0 %fusion.74 = f32[4,3,128,512]{3,2,1,0:T(8,128)} fusion(f32[16,4,3,128,512]{4,3,2,1,0:T(8,128)} %get-tuple-element.323, s32[]{:T(128)S(6)} %select_n.127, f32[4,3,128,512]{3,2,1,0:T(8,128)} %get-tuple-element.310, f32[4,3,128]{2,1,0:T(4,128)S(1)} %get-tuple-element.295, f32[4,3,128]{2,1,0:T(4,128)S(1)} %get-tuple-element.296), kind=kLoop, calls=%fused_computation.1.clone.1 | loop fusion | flops 2359296 | bytes 9449476 | tf_op jit(solution)/shard_map/while/body/eval_jaxpr/add | solution.py:39
  387.3 5.0 %fusion.74 = f32[4,3,128,512]{3,2,1,0:T(8,128)} fusion(f32[16,4,3,128,512]{4,3,2,1,0:T(8,128)} %get-tuple-element.323, s32[]{:T(128)S(6)} %select_n.127, f32[4,3,128,512]{3,2,1,0:T(8,128)} %get-tuple-element.310, f32[4,3,128]{2,1,0:T(4,128)S(1)} %get-tuple-element.295, f32[4,3,128]{2,1,0:T(4,128)S(1)} %get-tuple-element.296), kind=kLoop, calls=%fused_computation.1.clone.1 | loop fusion | flops 2359296 | bytes 9449476 | tf_op jit(solution)/shard_map/while/body/eval_jaxpr/add | solution.py:39
  392.3 5.0 %fusion.74 = f32[4,3,128,512]{3,2,1,0:T(8,128)} fusion(f32[16,4,3,128,512]{4,3,2,1,0:T(8,128)} %get-tuple-element.323, s32[]{:T(128)S(6)} %select_n.127, f32[4,3,128,512]{3,2,1,0:T(8,128)} %get-tuple-element.310, f32[4,3,128]{2,1,0:T(4,128)S(1)} %get-tuple-element.295, f32[4,3,128]{2,1,0:T(4,128)S(1)} %get-tuple-element.296), kind=kLoop, calls=%fused_computation.1.clone.1 | loop fusion | flops 2359296 | bytes 9449476 | tf_op jit(solution)/shard_map/while/body/eval_jaxpr/add | solution.py:39
  397.3 5.0 %fusion.74 = f32[4,3,128,512]{3,2,1,0:T(8,128)} fusion(f32[16,4,3,128,512]{4,3,2,1,0:T(8,128)} %get-tuple-element.323, s32[]{:T(128)S(6)} %select_n.127, f32[4,3,128,512]{3,2,1,0:T(8,128)} %get-tuple-element.310, f32[4,3,128]{2,1,0:T(4,128)S(1)} %get-tuple-element.295, f32[4,3,128]{2,1,0:T(4,128)S(1)} %get-tuple-element.296), kind=kLoop, calls=%fused_computation.1.clone.1 | loop fusion | flops 2359296 | bytes 9449476 | tf_op jit(solution)/shard_map/while/body/eval_jaxpr/add | solution.py:39
  402.3 5.0 %fusion.74 = f32[4,3,128,512]{3,2,1,0:T(8,128)} fusion(f32[16,4,3,128,512]{4,3,2,1,0:T(8,128)} %get-tuple-element.323, s32[]{:T(128)S(6)} %select_n.127, f32[4,3,128,512]{3,2,1,0:T(8,128)} %get-tuple-element.310, f32[4,3,128]{2,1,0:T(4,128)S(1)} %get-tuple-element.295, f32[4,3,128]{2,1,0:T(4,128)S(1)} %get-tuple-element.296), kind=kLoop, calls=%fused_computation.1.clone.1 | loop fusion | flops 2359296 | bytes 9449476 | tf_op jit(solution)/shard_map/while/body/eval_jaxpr/add | solution.py:39
  407.3 5.0 %fusion.74 = f32[4,3,128,512]{3,2,1,0:T(8,128)} fusion(f32[16,4,3,128,512]{4,3,2,1,0:T(8,128)} %get-tuple-element.323, s32[]{:T(128)S(6)} %select_n.127, f32[4,3,128,512]{3,2,1,0:T(8,128)} %get-tuple-element.310, f32[4,3,128]{2,1,0:T(4,128)S(1)} %get-tuple-element.295, f32[4,3,128]{2,1,0:T(4,128)S(1)} %get-tuple-element.296), kind=kLoop, calls=%fused_computation.1.clone.1 | loop fusion | flops 2359296 | bytes 9449476 | tf_op jit(solution)/shard_map/while/body/eval_jaxpr/add | solution.py:39
  412.4 5.0 %fusion.74 = f32[4,3,128,512]{3,2,1,0:T(8,128)} fusion(f32[16,4,3,128,512]{4,3,2,1,0:T(8,128)} %get-tuple-element.323, s32[]{:T(128)S(6)} %select_n.127, f32[4,3,128,512]{3,2,1,0:T(8,128)} %get-tuple-element.310, f32[4,3,128]{2,1,0:T(4,128)S(1)} %get-tuple-element.295, f32[4,3,128]{2,1,0:T(4,128)S(1)} %get-tuple-element.296), kind=kLoop, calls=%fused_computation.1.clone.1 | loop fusion | flops 2359296 | bytes 9449476 | tf_op jit(solution)/shard_map/while/body/eval_jaxpr/add | solution.py:39
  417.4 5.0 %fusion.74 = f32[4,3,128,512]{3,2,1,0:T(8,128)} fusion(f32[16,4,3,128,512]{4,3,2,1,0:T(8,128)} %get-tuple-element.323, s32[]{:T(128)S(6)} %select_n.127, f32[4,3,128,512]{3,2,1,0:T(8,128)} %get-tuple-element.310, f32[4,3,128]{2,1,0:T(4,128)S(1)} %get-tuple-element.295, f32[4,3,128]{2,1,0:T(4,128)S(1)} %get-tuple-element.296), kind=kLoop, calls=%fused_computation.1.clone.1 | loop fusion | flops 2359296 | bytes 9449476 | tf_op jit(solution)/shard_map/while/body/eval_jaxpr/add | solution.py:39
  422.4 5.0 %fusion.74 = f32[4,3,128,512]{3,2,1,0:T(8,128)} fusion(f32[16,4,3,128,512]{4,3,2,1,0:T(8,128)} %get-tuple-element.323, s32[]{:T(128)S(6)} %select_n.127, f32[4,3,128,512]{3,2,1,0:T(8,128)} %get-tuple-element.310, f32[4,3,128]{2,1,0:T(4,128)S(1)} %get-tuple-element.295, f32[4,3,128]{2,1,0:T(4,128)S(1)} %get-tuple-element.296), kind=kLoop, calls=%fused_computation.1.clone.1 | loop fusion | flops 2359296 | bytes 9449476 | tf_op jit(solution)/shard_map/while/body/eval_jaxpr/add | solution.py:39
  427.4 5.0 %fusion.74 = f32[4,3,128,512]{3,2,1,0:T(8,128)} fusion(f32[16,4,3,128,512]{4,3,2,1,0:T(8,128)} %get-tuple-element.323, s32[]{:T(128)S(6)} %select_n.127, f32[4,3,128,512]{3,2,1,0:T(8,128)} %get-tuple-element.310, f32[4,3,128]{2,1,0:T(4,128)S(1)} %get-tuple-element.295, f32[4,3,128]{2,1,0:T(4,128)S(1)} %get-tuple-element.296), kind=kLoop, calls=%fused_computation.1.clone.1 | loop fusion | flops 2359296 | bytes 9449476 | tf_op jit(solution)/shard_map/while/body/eval_jaxpr/add | solution.py:39
  432.4 5.0 %fusion.74 = f32[4,3,128,512]{3,2,1,0:T(8,128)} fusion(f32[16,4,3,128,512]{4,3,2,1,0:T(8,128)} %get-tuple-element.323, s32[]{:T(128)S(6)} %select_n.127, f32[4,3,128,512]{3,2,1,0:T(8,128)} %get-tuple-element.310, f32[4,3,128]{2,1,0:T(4,128)S(1)} %get-tuple-element.295, f32[4,3,128]{2,1,0:T(4,128)S(1)} %get-tuple-element.296), kind=kLoop, calls=%fused_computation.1.clone.1 | loop fusion | flops 2359296 | bytes 9449476 | tf_op jit(solution)/shard_map/while/body/eval_jaxpr/add | solution.py:39
  437.4 5.0 %fusion.74 = f32[4,3,128,512]{3,2,1,0:T(8,128)} fusion(f32[16,4,3,128,512]{4,3,2,1,0:T(8,128)} %get-tuple-element.323, s32[]{:T(128)S(6)} %select_n.127, f32[4,3,128,512]{3,2,1,0:T(8,128)} %get-tuple-element.310, f32[4,3,128]{2,1,0:T(4,128)S(1)} %get-tuple-element.295, f32[4,3,128]{2,1,0:T(4,128)S(1)} %get-tuple-element.296), kind=kLoop, calls=%fused_computation.1.clone.1 | loop fusion | flops 2359296 | bytes 9449476 | tf_op jit(solution)/shard_map/while/body/eval_jaxpr/add | solution.py:39
  442.4 5.0 %fusion.74 = f32[4,3,128,512]{3,2,1,0:T(8,128)} fusion(f32[16,4,3,128,512]{4,3,2,1,0:T(8,128)} %get-tuple-element.323, s32[]{:T(128)S(6)} %select_n.127, f32[4,3,128,512]{3,2,1,0:T(8,128)} %get-tuple-element.310, f32[4,3,128]{2,1,0:T(4,128)S(1)} %get-tuple-element.295, f32[4,3,128]{2,1,0:T(4,128)S(1)} %get-tuple-element.296), kind=kLoop, calls=%fused_computation.1.clone.1 | loop fusion | flops 2359296 | bytes 9449476 | tf_op jit(solution)/shard_map/while/body/eval_jaxpr/add | solution.py:39
  447.4 5.0 %fusion.74 = f32[4,3,128,512]{3,2,1,0:T(8,128)} fusion(f32[16,4,3,128,512]{4,3,2,1,0:T(8,128)} %get-tuple-element.323, s32[]{:T(128)S(6)} %select_n.127, f32[4,3,128,512]{3,2,1,0:T(8,128)} %get-tuple-element.310, f32[4,3,128]{2,1,0:T(4,128)S(1)} %get-tuple-element.295, f32[4,3,128]{2,1,0:T(4,128)S(1)} %get-tuple-element.296), kind=kLoop, calls=%fused_computation.1.clone.1 | loop fusion | flops 2359296 | bytes 9449476 | tf_op jit(solution)/shard_map/while/body/eval_jaxpr/add | solution.py:39
  452.4 5.0 %fusion.74 = f32[4,3,128,512]{3,2,1,0:T(8,128)} fusion(f32[16,4,3,128,512]{4,3,2,1,0:T(8,128)} %get-tuple-element.323, s32[]{:T(128)S(6)} %select_n.127, f32[4,3,128,512]{3,2,1,0:T(8,128)} %get-tuple-element.310, f32[4,3,128]{2,1,0:T(4,128)S(1)} %get-tuple-element.295, f32[4,3,128]{2,1,0:T(4,128)S(1)} %get-tuple-element.296), kind=kLoop, calls=%fused_computation.1.clone.1 | loop fusion | flops 2359296 | bytes 9449476 | tf_op jit(solution)/shard_map/while/body/eval_jaxpr/add | solution.py:39
  (102 shorter events, 22.8 us)
Async XLA Ops:
  6.5 1.2 copy-start
  6.5 67.1 %all-gather.3.cloned.1.call-start = ((), (), s32[]{:S(2)}) async-start(), calls=%async_computation.2 | async-start | bytes 2088960 | tf_op jit(solution)/shard_map/all_gather | solution.py:52
  11.9 17.3 %all-to-all-start = ((bf16[8,2,1]{1,2,0:T(2,128)(2,1)}), bf16[8,2,1]{1,2,0:T(2,128)(2,1)S(1)}, u32[]{:S(2)}, u32[]{:S(2)}) async-start(bf16[8,2,1]{1,2,0:T(2,128)(2,1)} %convert_element_type.64), calls=%async_computation | async-start | bytes 8192 | tf_op jit(solution)/shard_map/all_to_all | solution.py:89
  26.6 7.6 %copy-start.8 = (s32[2]{0:T(128)S(1)}, s32[2]{0:T(128)}, u32[]{:S(2)}) copy-start(s32[2]{0:T(128)} %param.16) | copy-start | bytes 28
  29.2 34.8 %all-to-all-start.1 = ((bf16[16,128,576]{1,2,0:T(8,128)(2,1)}), bf16[16,128,576]{1,2,0:T(8,128)(2,1)S(1)}, u32[]{:S(2)}, u32[]{:S(2)}) async-start(bf16[16,128,576]{1,2,0:T(8,128)(2,1)} %copy.65), calls=%async_computation.1 | async-start | bytes 4718592 | tf_op jit(solution)/shard_map/all_to_all | solution.py:88
  34.0 344.4 %all-gather.5.cloned.1.call-start = ((), (), s32[]{:S(2)}) async-start(), calls=%async_computation.3 | async-start | bytes 53477376 | tf_op jit(solution)/shard_map/all_gather | solution.py:15
  77.6 5.3 %slice-start = ((s8[4718592]{0:T(1024)(128)(4,1)}), s8[4194304]{0:T(1024)(128)(4,1)S(1)}, s32[]{:S(2)}) async-start(s8[4718592]{0:T(1024)(128)(4,1)} %bitcast.96), calls=%async_computation.4 | async-start | bytes 8388608
  77.7 5.2 %slice-start.1 = ((s8[4718592]{0:T(1024)(128)(4,1)}), s8[524288]{0:T(1024)(128)(4,1)S(1)}, s32[]{:S(2)}) async-start(s8[4718592]{0:T(1024)(128)(4,1)} %bitcast.96), calls=%async_computation.5 | async-start | bytes 1048576
  82.9 3.0 copy-start.2
  82.9 3.4 copy-start.5
  86.4 2.9 copy-start.4
  89.2 2.6 copy-start.3
  91.8 2.1 copy-start.7
  91.8 2.2 copy-start.6
  382.2 76.6 %copy-start.9 = (bf16[8,512,128]{2,1,0:T(8,128)(2,1)S(1)}, bf16[8,512,128]{2,1,0:T(8,128)(2,1)}, u32[]{:S(2)}) copy-start(bf16[8,512,128]{2,1,0:T(8,128)(2,1)} %param.14) | copy-start | bytes 3145732
  457.4 2.3 copy-start.1
Sparse Core Ops, SparseCore 0:
  9.6 47.1 all-gather.2
  94.1 284.2 all-gather.4
where the time goes:
time: 468 us; the launch traced here: 467 us
  waiting for transfers between devices  259 us (55%)
  other arithmetic  86.4 us (18%)
  blocking collectives  48.3 us (10%)
  local copies, waits for them, and re-layouts  32.9 us (7%)
  matrix products  17.1 us (4%)
  between operations  13.7 us (3%)
  starting transfers between devices  9.55 us (2%)
    all_gather x1, waiting for transfers between devices, merged(): gathered = jax.tree.map(lambda a: lax.all_gather(a, axis), part)  229 us
    add x15, other arithmetic, combine_two(): weighted_first * keep_first[..., None]  74.7 us
    all_gather x2, blocking collectives, merged(): gathered = jax.tree.map(lambda a: lax.all_gather(a, axis), part)  48.3 us
    all_to_all x1, waiting for transfers between devices, body(): lax.all_to_all(send_rows, 'group', split_axis=0, concat_axis=0, tiled=True)  29.4 us
  transfers between devices with their start and end apart: 4, of which 2 were waited for; matrix products, arithmetic and copies ran while one was open for 7% of the time, Pallas kernels for 0%

commit v1 on v0

v1 whole, which is shorter than its diff:
```python
import math

import jax
import jax.numpy as jnp
from jax import lax
from jax.experimental import pallas as pl
from jax.experimental.pallas import tpu as pltpu
from jax.sharding import PartitionSpec as P

MESH = pl.DeviceIdType.MESH
F32 = jnp.float32
BF16 = jnp.bfloat16

NY, NC, NZ, NX = 4, 2, 4, 4
HEADS = 8
STEPS = 3
PART = STEPS * HEADS
ROWS = 2 * PART
NSEQ = NZ * NX
QROWS = NSEQ * PART
LAT, ROPE = 512, 64
BLK = 128
CTX = 2048
QMSG = 5 * ROWS
QCUT = 128
PMSG = 4 * ROWS + 16
KMSG = 8 * BLK + BLK + 16
NEG = -1e30
EXPC = (128 + 64) ** -0.5 * math.log2(math.e)

GROUP = [(0, 0), (0, 1), (1, 0), (1, 1), (3, 0), (3, 1), (2, 0), (2, 1)]


def dot_t(a, b):
    return lax.dot_general(a, b, (((1,), (1,)), ((), ())), preferred_element_type=F32)


def dot(a, b):
    return jnp.dot(a, b, preferred_element_type=F32)


def kernel(
    qn_ref, qr_ref, wa_hbm, wv_hbm, cache_hbm, len_ref, pre_hbm, dest_ref, new_ref,
    out_ref,
    wa, wv, cache, pre, ysend, kv, qbuf, qall, scores, weights, acc, peak, total,
    fresh, fresh_w, fresh_m, fresh_l, pout, pin,
    local_sem, y_ss, y_rs, a_ss, a_rs, f_ss, f_rs, p_ss, p_rs,
):
    g, s = lax.axis_index("group"), lax.axis_index("seq")
    y, c = lax.div(g, NC), lax.rem(g, NC)
    z, x = lax.div(s, NX), lax.rem(s, NX)

    def group_of(dy, dc):
        return lax.rem(y + dy, NY) * NC + lax.rem(c + dc, NC)

    def seq_dev(dz, dx):
        return (g, lax.rem(z + dz, NZ) * NX + lax.rem(x + dx, NX))

    loads = [
        pltpu.make_async_copy(src, dst, local_sem.at[i])
        for i, (src, dst) in enumerate(
            [(pre_hbm.at[0], pre), (wa_hbm, wa), (cache_hbm, cache), (wv_hbm, wv)]
        )
    ]
    for load in loads:
        load.start()

    barrier = pltpu.get_barrier_semaphore()
    for dy, dc in GROUP[1:]:
        pl.semaphore_signal(barrier, inc=1, device_id=(group_of(dy, dc), s), device_id_type=MESH)
    for j in range(1, NSEQ):
        pl.semaphore_signal(
            barrier, inc=1, device_id=seq_dev(j // NX, j % NX), device_id_type=MESH
        )

    owners = [dest_ref[0, k] for k in range(8)]
    targets = [lax.div(o, 2) for o in owners]
    members = [lax.rem(o, 2) for o in owners]
    loads[0].wait()
    tag_row = lax.broadcasted_iota(jnp.int32, (16, 128), 0)
    for i, (dy, dc) in enumerate(GROUP):
        wanted = group_of(dy, dc)
        first = second = jnp.int32(0)
        tag_first = tag_second = jnp.int32(2)
        for k in reversed(range(8)):
            match = targets[k] == wanted
            second = jnp.where(match, first, second)
            tag_second = jnp.where(match, tag_first, tag_second)
            first = jnp.where(match, k, first)
            tag_first = jnp.where(match, members[k], tag_first)
        to = kv if i == 0 else ysend
        for slot, index in enumerate((first, second)):
            for p in range(4):
                to[i, pl.ds(p * 2 * BLK + slot * BLK, BLK), :] = pre[
                    index, :, p * 128 : (p + 1) * 128
                ]
        to[i, pl.ds(8 * BLK, BLK), :] = jnp.concatenate(
            [pre[first, :, LAT : LAT + ROPE], pre[second, :, LAT : LAT + ROPE]], axis=1
        )
        tags = jnp.where(tag_row < 8, tag_first, tag_second)
        to[i, pl.ds(9 * BLK, 16), :] = tags.astype(F32).astype(BF16)

    loads[1].wait()
    row = lax.broadcasted_iota(jnp.int32, (2 * ROWS, 128), 0)
    own = qn_ref[...].astype(F32)
    spread = [jnp.where((row & 7) == h, own, 0.0).astype(BF16) for h in range(HEADS)]
    q_latent = dot(jnp.concatenate(spread, axis=1), wa[...].reshape(HEADS * 128, LAT))
    q_latent = q_latent.astype(BF16)
    q_rope = jnp.concatenate([qr_ref[...], jnp.zeros((2 * ROWS, 128 - ROPE), BF16)], axis=1)
    for pair in range(2):
        rows = slice(pair * ROWS, (pair + 1) * ROWS)
        for p in range(4):
            qbuf[pair, 0, 0, pl.ds(p * ROWS, ROWS), :] = q_latent[rows, p * 128 : (p + 1) * 128]
        qbuf[pair, 0, 0, pl.ds(4 * ROWS, ROWS), :] = q_rope[rows]

    pl.semaphore_wait(barrier, 7 + NSEQ - 1)

    def group_copy(i):
        dy, dc = GROUP[i]
        there = GROUP.index(((NY - dy) % NY, dc))
        return pltpu.make_async_remote_copy(
            src_ref=ysend.at[i], dst_ref=kv.at[there], send_sem=y_ss.at[i], recv_sem=y_rs.at[there],
            device_id=(group_of(dy, dc), s), device_id_type=MESH,
        )

    group_copies = [group_copy(i) for i in range(1, 8)]
    for copy in group_copies:
        copy.start()

    low, high = pl.ds(0, QCUT), pl.ds(QCUT, QMSG - QCUT)

    def own_copy(pair, index, dz, dx, rows):
        return pltpu.make_async_remote_copy(
            src_ref=qbuf.at[pair, 0, 0, rows], dst_ref=qbuf.at[pair, (NZ - dz) % NZ, (NX - dx) % NX, rows],
            send_sem=a_ss.at[pair, index], recv_sem=a_rs.at[pair, index],
            device_id=seq_dev(dz, dx), device_id_type=MESH,
        )

    def x_first(pair):
        return [own_copy(pair, d - 1, 0, d, low) for d in (1, 2, 3)]

    def z_first(pair):
        return [own_copy(pair, 2 + d, d, 0, high) for d in (1, 2, 3)]

    def rest(pair):
        return [own_copy(pair, 5 + d, 0, d, high) for d in (1, 2, 3)] + [
            own_copy(pair, 8 + d, d, 0, low) for d in (1, 2, 3)
        ]

    def forward_z(pair):
        return [
            pltpu.make_async_remote_copy(
                src_ref=qbuf.at[pair, 0, pl.ds(1, 3), low], dst_ref=qbuf.at[pair, NZ - d, pl.ds(1, 3), low],
                send_sem=f_ss.at[pair, d - 1], recv_sem=f_rs.at[pair, d - 1],
                device_id=seq_dev(d, 0), device_id_type=MESH,
            )
            for d in (1, 2, 3)
        ]

    def forward_x(pair):
        return [
            pltpu.make_async_remote_copy(
                src_ref=qbuf.at[pair, pl.ds(1, 3), 0, high], dst_ref=qbuf.at[pair, pl.ds(1, 3), NX - d, high],
                send_sem=f_ss.at[pair, 2 + d], recv_sem=f_rs.at[pair, 2 + d],
                device_id=seq_dev(0, d), device_id_type=MESH,
            )
            for d in (1, 2, 3)
        ]

    def start(copies):
        for copy in copies:
            copy.start()
        return copies

    def arrived(copies):
        for copy in copies:
            copy.wait_recv()

    sent = []
    first_x, first_z = start(x_first(0)), start(z_first(0))
    others = start(rest(0))
    sent += first_x + first_z + others

    fresh[...] = jnp.zeros_like(fresh)
    for r in range(4):
        fresh[pl.ds(8 * r, STEPS), :] = new_ref[r].astype(F32)
    fresh_rows = fresh[...].astype(BF16)
    s_fresh = dot_t(q_latent, fresh_rows[:, :LAT]) + dot_t(
        qr_ref[...], fresh_rows[:, LAT : LAT + ROPE]
    )
    part = lax.broadcasted_iota(jnp.int32, (2 * ROWS, 32), 0) >> 3
    key = lax.broadcasted_iota(jnp.int32, (2 * ROWS, 32), 1)
    request = (
        (part >= 3).astype(jnp.int32) + (part >= 6).astype(jnp.int32) + (part >= 9).astype(jnp.int32)
    )
    step = part - 3 * request
    allowed = ((key >> 3) == request) & ((key & 7) <= step)
    s_fresh = jnp.where(allowed, s_fresh, NEG)
    m_fresh = jnp.max(s_fresh, axis=1, keepdims=True)
    p_fresh = jnp.where(allowed, jnp.exp2((s_fresh - m_fresh) * EXPC), 0.0)
    fresh_m[...] = jnp.broadcast_to(m_fresh, fresh_m.shape)
    fresh_l[...] = jnp.broadcast_to(jnp.sum(p_fresh, axis=1, keepdims=True), fresh_l.shape)
    fresh_w[...] = dot(p_fresh.astype(BF16), fresh_rows[:, :LAT])

    arrived(first_x)
    sent += (forward_z0 := start(forward_z(0)))
    arrived(first_z)
    sent += (forward_x0 := start(forward_x(0)))
    first_x1, first_z1 = start(x_first(1)), start(z_first(1))
    others1 = start(rest(1))
    sent += first_x1 + first_z1 + others1
    arrived(first_x1)
    sent += (forward_z1 := start(forward_z(1)))
    arrived(first_z1)
    sent += (forward_x1 := start(forward_x(1)))

    def assemble(pair):
        def two(i, carry):
            at = pl.multiple_of(i * 2 * PART, 16)
            dz, dx = lax.div(i, 2), lax.rem(i, 2) * 2
            for p in range(5):
                one = qbuf[pair, dz, dx, pl.ds(p * ROWS, ROWS), :].astype(F32)
                two = qbuf[pair, dz, dx + 1, pl.ds(p * ROWS, ROWS), :].astype(F32)
                lanes = slice(p * 128, (p + 1) * 128)
                for r in range(2):
                    rows = slice(r * PART, (r + 1) * PART)
                    qall[2 * pair + r, pl.ds(at, 2 * PART), lanes] = jnp.concatenate(
                        [one[rows], two[rows]], axis=0
                    ).astype(BF16)
            return carry

        lax.fori_loop(0, NSEQ // 2, two, 0)

    def pack(pair):
        lane = lax.broadcasted_iota(jnp.int32, (16, 128), 1)

        def one(j, carry):
            at = pl.multiple_of(j * PART, 8)

            def both(ref):
                return jnp.concatenate(
                    [ref[2 * pair, pl.ds(at, PART), :], ref[2 * pair + 1, pl.ds(at, PART), :]], axis=0
                )

            for p in range(4):
                lanes = slice(p * 128, (p + 1) * 128)
                pout[pair, j, pl.ds(p * ROWS, ROWS), :] = jnp.concatenate(
                    [acc[2 * pair, pl.ds(at, PART), lanes], acc[2 * pair + 1, pl.ds(at, PART), lanes]],
                    axis=0,
                ).astype(BF16)
            m, l = both(peak), both(total)
            m_high = m.astype(BF16).astype(F32)
            m_mid = (m - m_high).astype(BF16).astype(F32)
            m_low = m - m_high - m_mid
            l_high = l.astype(BF16).astype(F32)
            stats = jnp.zeros((16, 128), F32)
            for i in range(3):
                rows = slice(16 * i, 16 * (i + 1))
                for q, value in enumerate((m_high, m_mid, m_low, l_high, l - l_high)):
                    stats = jnp.where(lane == 8 * i + q, value[rows], stats)
            pout[pair, j, pl.ds(4 * ROWS, 16), :] = stats.astype(BF16)
            return carry

        lax.fori_loop(0, NSEQ, one, 0)

    def partial_copies(pair):
        return [
            pltpu.make_async_remote_copy(
                src_ref=pout.at[pair, j], dst_ref=pin.at[pair, (NZ - j // NX) % NZ * NX + (NX - j % NX) % NX],
                send_sem=p_ss.at[pair, j], recv_sem=p_rs.at[pair, j],
                device_id=seq_dev(j // NX, j % NX), device_id_type=MESH,
            )
            for j in range(1, NSEQ)
        ]

    def finish(pair):
        stats = jnp.concatenate(
            [pout[pair, 0, pl.ds(4 * ROWS, 16), :]]
            + [pin[pair, j, pl.ds(4 * ROWS, 16), :] for j in range(1, NSEQ)],
            axis=0,
        )
        source = lax.broadcasted_iota(jnp.int32, (128, 128), 0)
        picks = [
            ((source >= 8 * i) & (source < 8 * i + 3)).astype(F32).astype(BF16) for i in range(3)
        ] + [
            ((source >= 8 * i + 3) & (source < 8 * i + 5)).astype(F32).astype(BF16) for i in range(3)
        ]
        spread_stats = dot(stats, jnp.concatenate(picks, axis=1))

        def of(j, kind):
            return jnp.concatenate(
                [
                    spread_stats[16 * j : 16 * (j + 1), 128 * (3 * kind + i) : 128 * (3 * kind + i + 1)]
                    for i in range(3)
                ],
                axis=0,
            )

        rows = pl.ds(pair * ROWS, ROWS)
        peaks = [of(j, 0) for j in range(NSEQ)]
        m_fresh = fresh_m[rows, :]
        top = m_fresh
        for m in peaks:
            top = jnp.maximum(top, m)
        keep = jnp.exp2((m_fresh - top) * EXPC)
        sums = keep * fresh_l[rows, :]
        values = [keep * fresh_w[rows, p * 128 : (p + 1) * 128] for p in range(4)]
        for j in range(NSEQ):
            keep = jnp.exp2((peaks[j] - top) * EXPC)
            sums = sums + keep * of(j, 1)
            message = pout if j == 0 else pin
            for p in range(4):
                values[p] = values[p] + keep * message[pair, j, pl.ds(p * ROWS, ROWS), :].astype(F32)
        head = lax.broadcasted_iota(jnp.int32, (ROWS, 128), 0) & 7
        attended = [(v / sums).astype(BF16).astype(F32) for v in values]
        spread = [
            jnp.where(head == h, attended[p], 0.0).astype(BF16) for h in range(HEADS) for p in range(4)
        ]
        result = dot(jnp.concatenate(spread, axis=1), wv[...].reshape(HEADS * LAT, 128))
        out_ref[rows, :] = result.astype(BF16)

    arrived(others + forward_z0 + forward_x0)
    assemble(0)
    loads[2].wait()

    def resident(r, carry):
        limit = len_ref[r] - s * CTX
        tile = 512
        position = lax.broadcasted_iota(jnp.int32, (QROWS, tile), 1)
        running = jnp.full((QROWS, 128), NEG, F32)
        for k in range(CTX // tile):
            keys = pl.ds(k * tile, tile)
            sc = dot_t(qall[r, :, :LAT], cache[r, keys, :LAT]) + dot_t(
                qall[r, :, LAT : LAT + ROPE], cache[r, keys, LAT : LAT + ROPE]
            )
            sc = jnp.where(position < limit - k * tile, sc, NEG)
            scores[:, keys] = sc
            for i in range(tile // 128):
                running = jnp.maximum(running, sc[:, i * 128 : (i + 1) * 128])
        m = jnp.max(running, axis=1, keepdims=True)
        sums = jnp.zeros((QROWS, 128), F32)
        for k in range(CTX // tile):
            keys = pl.ds(k * tile, tile)
            w = jnp.exp2((scores[:, keys] - m) * EXPC)
            for i in range(tile // 128):
                sums = sums + w[:, i * 128 : (i + 1) * 128]
            weights[:, keys] = w.astype(BF16)
        acc[r] = dot(weights[...], cache[r, :, :LAT])
        peak[r] = jnp.broadcast_to(m, (QROWS, 128))
        total[r] = jnp.broadcast_to(jnp.sum(sums, axis=1, keepdims=True), (QROWS, 128))
        return carry

    lax.fori_loop(0, 2, resident, 0)
    pack(0)
    partials0 = start(partial_copies(0))

    arrived(others1 + forward_z1 + forward_x1)
    assemble(1)
    for r in (2, 3):
        acc[r] = jnp.zeros((QROWS, LAT), F32)
        peak[r] = jnp.full((QROWS, 128), NEG, F32)
        total[r] = jnp.zeros((QROWS, 128), F32)

    def blocks(i):
        latent = jnp.concatenate(
            [kv[i, pl.ds(p * 2 * BLK, 2 * BLK), :] for p in range(4)], axis=1
        )
        ropes = kv[i, pl.ds(8 * BLK, BLK), :]
        tags = kv[i, pl.ds(9 * BLK, 16), :].astype(F32)
        tag = jnp.concatenate([tags[0:1, :], tags[8:9, :]], axis=1)
        for r in (2, 3):
            q_rope = qall[r, :, LAT : LAT + ROPE]
            sc = dot_t(qall[r, :, :LAT], latent) + jnp.concatenate(
                [dot_t(q_rope, ropes[:, :ROPE]), dot_t(q_rope, ropes[:, ROPE:])], axis=1
            )
            sc = jnp.where(tag == float(r - 2), sc, NEG)
            old = peak[r]
            best = jnp.max(
                jnp.maximum(sc[:, :128], sc[:, 128:]), axis=1, keepdims=True
            )
            top = jnp.maximum(old, best)
            keep = jnp.exp2((old - top) * EXPC)
            w0 = jnp.exp2((sc[:, :128] - top) * EXPC)
            w1 = jnp.exp2((sc[:, 128:] - top) * EXPC)
            peak[r] = top
            total[r] = total[r] * keep + jnp.sum(w0 + w1, axis=1, keepdims=True)
            w = jnp.concatenate([w0, w1], axis=1).astype(BF16)
            term = dot(w, latent)
            for p in range(4):
                lanes = slice(p * 128, (p + 1) * 128)
                acc[r, :, lanes] = acc[r, :, lanes] * keep + term[:, lanes]

    def landed(i, carry):
        pltpu.make_async_remote_copy(
            src_ref=ysend.at[i], dst_ref=kv.at[i], send_sem=y_ss.at[i], recv_sem=y_rs.at[i],
            device_id=(group_of(0, 1), s), device_id_type=MESH,
        ).wait_recv()
        blocks(i)
        return carry

    blocks(0)
    lax.fori_loop(1, 6, landed, 0)
    loads[3].wait()
    arrived(partials0)
    finish(0)
    lax.fori_loop(6, 8, landed, 0)
    pack(1)
    partials1 = start(partial_copies(1))
    arrived(partials1)
    finish(1)
    for copy in group_copies + sent + partials0 + partials1:
        copy.wait_send()


def body(q_nope, q_rope, w_absorb, w_value, cache, res_len, prefill_rows, block_dest, new_rows):
    rows = 4 * PART
    vmem, hbm, smem = (
        pl.BlockSpec(memory_space=pltpu.VMEM),
        pl.BlockSpec(memory_space=pl.ANY),
        pl.BlockSpec(memory_space=pltpu.SMEM),
    )
    out = pl.pallas_call(
        kernel,
        out_shape=jax.ShapeDtypeStruct((rows, 128), BF16),
        in_specs=[vmem, vmem, hbm, hbm, hbm, smem, hbm, smem, vmem],
        out_specs=vmem,
        scratch_shapes=[
            pltpu.VMEM(w_absorb.shape, BF16),
            pltpu.VMEM(w_value.shape, BF16),
            pltpu.VMEM(cache.shape, BF16),
            pltpu.VMEM(prefill_rows.shape[1:], BF16),
            pltpu.VMEM((8, KMSG, 128), BF16),
            pltpu.VMEM((8, KMSG, 128), BF16),
            pltpu.VMEM((2, NZ, NX, QMSG, 128), BF16),
            pltpu.VMEM((4, QROWS, LAT + 128), BF16),
            pltpu.VMEM((QROWS, CTX), F32),
            pltpu.VMEM((QROWS, CTX), BF16),
            pltpu.VMEM((4, QROWS, LAT), F32),
            pltpu.VMEM((4, QROWS, 128), F32),
            pltpu.VMEM((4, QROWS, 128), F32),
            pltpu.VMEM((32, LAT + ROPE), F32),
            pltpu.VMEM((rows, LAT), F32),
            pltpu.VMEM((rows, 128), F32),
            pltpu.VMEM((rows, 128), F32),
            pltpu.VMEM((2, NSEQ, PMSG, 128), BF16),
            pltpu.VMEM((2, NSEQ, PMSG, 128), BF16),
            pltpu.SemaphoreType.DMA((4,)),
            pltpu.SemaphoreType.DMA((8,)),
            pltpu.SemaphoreType.DMA((8,)),
            pltpu.SemaphoreType.DMA((2, 12)),
            pltpu.SemaphoreType.DMA((2, 12)),
            pltpu.SemaphoreType.DMA((2, 6)),
            pltpu.SemaphoreType.DMA((2, 6)),
            pltpu.SemaphoreType.DMA((2, NSEQ)),
            pltpu.SemaphoreType.DMA((2, NSEQ)),
        ],
        compiler_params=pltpu.CompilerParams(
            collective_id=0, has_side_effects=True, vmem_limit_bytes=56 * 1024 * 1024
        ),
        name="latent_attention",
    )(
        q_nope.reshape(rows, 128),
        q_rope.reshape(rows, ROPE),
        w_absorb,
        w_value,
        cache,
        res_len,
        prefill_rows,
        block_dest,
        new_rows,
    )
    return out.reshape(q_nope.shape)


def solution(mesh):
    in_specs = (
        P("group", None, "seq", None),
        P("group", None, "seq", None),
        P("seq", None, None),
        P("seq", None, None),
        P("group", "seq", None),
        P("group"),
        P("group", "seq", None, None),
        P("group", "seq"),
        P("group", None, None),
    )
    out_specs = P("group", None, "seq", None)
    return jax.shard_map(body, mesh=mesh, in_specs=in_specs, out_specs=out_specs, check_vma=False)
```

time: 468 us -> 66.6 us (0.14)
  waiting for transfers between devices: 259 us -> 0 us
  other arithmetic: 86.4 us -> 0 us
  Pallas kernels: 0 us -> 53.4 us
  blocking collectives: 48.3 us -> 0 us
  local copies, waits for them, and re-layouts: 32.9 us -> 12.8 us
  matrix products: 17.1 us -> 0 us
  between operations: 13.7 us -> 0.01 us
  starting transfers between devices: 9.55 us -> 0 us
    all_gather x2 -> x0, waiting for transfers between devices: 229 us -> none  [the longest x1 229 us: merged(): gathered = jax.tree.map(lambda a: lax.all_gather(a, axis), part)]
    add x32 -> x0, other arithmetic: 75.2 us -> none  [the longest x15 74.7 us: combine_two(): weighted_first * keep_first[..., None]]
    pallas_call x0 -> x1, Pallas kernels: none -> 53.4 us  [body(): pl.pallas_call(kernel, out_shape=jax.ShapeDtypeStruct((rows, 128), BF16),...]
    all_gather x2 -> x0, blocking collectives: 48.3 us -> none  [merged(): gathered = jax.tree.map(lambda a: lax.all_gather(a, axis), part)]
    all_to_all x2 -> x0, waiting for transfers between devices: 29.4 us -> none  [the longest x1 29.4 us: body(): lax.all_to_all(send_rows, 'group', split_axis=0, concat_axis=0, tiled=True)]
    dot_general x9 -> x0, matrix products: 17.1 us -> none  [the longest x1 5.13 us: body(): jnp.einsum('rmk,rnk->rmn', flat_query[:RES], cache, preferred_element_typ...]
    reshape x4 -> x0, local copies, waits for them, and re-layouts: 13.7 us -> none  [the longest x2 7.01 us: body(): send_rows = send_rows.reshape(groups * CAP, block_rows, row_width)]
    all_to_all x2 -> x0, starting transfers between devices: 9.33 us -> none  [the longest x1 4.77 us: body(): lax.all_to_all(send_rows, 'group', split_axis=0, concat_axis=0, tiled=True)]
  transfers between devices with their start and end apart: 4 -> 0, of which waited for: 2 -> 0; matrix products, arithmetic and copies ran while one was open for 7% -> 0% of each run, Pallas kernels for 0% -> 0%
where the time goes in v1:
time: 66.6 us; the launch traced here: 66.2 us
  Pallas kernels  53.4 us (80%)
  local copies, waits for them, and re-layouts  12.8 us (19%)
    pallas_call x1, Pallas kernels, body(): pl.pallas_call(kernel, out_shape=jax.ShapeDtypeStruct((rows, 128), BF16),...  53.4 us
    unnamed x4, local copies, waits for them, and re-layouts  12.8 us

profile of v1, /device:TPU:0, one launch (start us, length us, event | category | flops | bytes accessed | tf_op | source)
XLA Modules:
  0.0 66.2 jit_solution(17483666223550948615)
XLA Ops:
  0.0 1.3 %copy.12.new_ref = bf16[4,3,576]{2,1,0:T(4,128)(2,1)} copy(bf16[4,3,576]{2,0,1:T(4,128)(2,1)} %param.17) | data formatting | bytes 27648 | tf_op args[8]
  1.3 2.4 %copy.11.pre_hbm = bf16[1,8,128,576]{3,2,1,0:T(8,128)(2,1)} copy(bf16[1,8,128,576]{2,3,1,0:T(8,128)(2,1)} %param.15) | data formatting | bytes 2359296 | tf_op args[6]
  3.7 7.7 %copy.10.cache_hbm = bf16[2,2048,576]{2,1,0:T(8,128)(2,1)} copy(bf16[2,2048,576]{1,2,0:T(8,128)(2,1)} %param.13) | data formatting | bytes 9437184 | tf_op args[4]
  11.4 53.4 %latent_attention.1 = bf16[96,128]{1,0:T(8,128)(2,1)} custom-call(bf16[96,128]{1,0:T(8,128)(2,1)} %bitcast.4, bf16[96,64]{1,0:T(8,128)(2,1)} %bitcast.5, bf16[8,128,512]{2,1,0:T(8,128)(2,1)} %wa_hbm.1, bf16[8,512,128]{2,1,0:T(8,128)(2,1)} %wv_hbm.1, bf16[2,2048,576]{2,1,0:T(8,128)(2,1)} %copy.10.cache_hbm, s32[2]{0:T(128)} %len_ref.1, ...), custom_call_target="tpu_custom_call" | custom-call | tf_op jit(solution)/shard_map/latent_attention/pallas_call | solution.py:422
  64.8 1.3 %copy.14 = bf16[4,3,8,128]{3,2,1,0:T(8,128)(2,1)} copy(bf16[4,3,8,128]{3,2,1,0:T(8,128)(2,1)} %bitcast.3) | data formatting | bytes 49152

commit v2 on v1

--- a/solution.py
+++ b/solution.py
@@ -24,7 +24,8 @@
 QMSG = 5 * ROWS
 QCUT = 128
 PMSG = 4 * ROWS + 16
-KMSG = 8 * BLK + BLK + 16
+ROW = LAT + ROPE
+KMSG = 2 * ROW + 16
 NEG = -1e30
 EXPC = (128 + 64) ** -0.5 * math.log2(math.e)
 
@@ -90,15 +91,9 @@
             tag_first = jnp.where(match, members[k], tag_first)
         to = kv if i == 0 else ysend
         for slot, index in enumerate((first, second)):
-            for p in range(4):
-                to[i, pl.ds(p * 2 * BLK + slot * BLK, BLK), :] = pre[
-                    index, :, p * 128 : (p + 1) * 128
-                ]
-        to[i, pl.ds(8 * BLK, BLK), :] = jnp.concatenate(
-            [pre[first, :, LAT : LAT + ROPE], pre[second, :, LAT : LAT + ROPE]], axis=1
-        )
+            to[i, pl.ds(slot * ROW, ROW), :] = pre[index]
         tags = jnp.where(tag_row < 8, tag_first, tag_second)
-        to[i, pl.ds(9 * BLK, 16), :] = tags.astype(F32).astype(BF16)
+        to[i, pl.ds(2 * ROW, 16), :] = tags.astype(F32).astype(BF16)
 
     loads[1].wait()
     row = lax.broadcasted_iota(jnp.int32, (2 * ROWS, 128), 0)
@@ -182,8 +177,10 @@
     sent += first_x + first_z + others
 
     fresh[...] = jnp.zeros_like(fresh)
-    for r in range(4):
-        fresh[pl.ds(8 * r, STEPS), :] = new_ref[r].astype(F32)
+    for u in range(STEPS):
+        new = new_ref[u].astype(F32)
+        for r in range(4):
+            fresh[pl.ds(8 * r + u, 1), :] = new[r : r + 1]
     fresh_rows = fresh[...].astype(BF16)
     s_fresh = dot_t(q_latent, fresh_rows[:, :LAT]) + dot_t(
         qr_ref[...], fresh_rows[:, LAT : LAT + ROPE]
@@ -330,9 +327,7 @@
         running = jnp.full((QROWS, 128), NEG, F32)
         for k in range(CTX // tile):
             keys = pl.ds(k * tile, tile)
-            sc = dot_t(qall[r, :, :LAT], cache[r, keys, :LAT]) + dot_t(
-                qall[r, :, LAT : LAT + ROPE], cache[r, keys, LAT : LAT + ROPE]
-            )
+            sc = dot(qall[r, :, :ROW], cache[r, :, keys])
             sc = jnp.where(position < limit - k * tile, sc, NEG)
             scores[:, keys] = sc
             for i in range(tile // 128):
@@ -345,7 +340,7 @@
             for i in range(tile // 128):
                 sums = sums + w[:, i * 128 : (i + 1) * 128]
             weights[:, keys] = w.astype(BF16)
-        acc[r] = dot(weights[...], cache[r, :, :LAT])
+        acc[r] = dot_t(weights[...], cache[r, :LAT, :])
         peak[r] = jnp.broadcast_to(m, (QROWS, 128))
         total[r] = jnp.broadcast_to(jnp.sum(sums, axis=1, keepdims=True), (QROWS, 128))
         return carry
@@ -362,17 +357,11 @@
         total[r] = jnp.zeros((QROWS, 128), F32)
 
     def blocks(i):
-        latent = jnp.concatenate(
-            [kv[i, pl.ds(p * 2 * BLK, 2 * BLK), :] for p in range(4)], axis=1
-        )
-        ropes = kv[i, pl.ds(8 * BLK, BLK), :]
-        tags = kv[i, pl.ds(9 * BLK, 16), :].astype(F32)
+        keys = jnp.concatenate([kv[i, pl.ds(0, ROW), :], kv[i, pl.ds(ROW, ROW), :]], axis=1)
+        tags = kv[i, pl.ds(2 * ROW, 16), :].astype(F32)
         tag = jnp.concatenate([tags[0:1, :], tags[8:9, :]], axis=1)
         for r in (2, 3):
-            q_rope = qall[r, :, LAT : LAT + ROPE]
-            sc = dot_t(qall[r, :, :LAT], latent) + jnp.concatenate(
-                [dot_t(q_rope, ropes[:, :ROPE]), dot_t(q_rope, ropes[:, ROPE:])], axis=1
-            )
+            sc = dot(qall[r, :, :ROW], keys)
             sc = jnp.where(tag == float(r - 2), sc, NEG)
             old = peak[r]
             best = jnp.max(
@@ -385,7 +374,7 @@
             peak[r] = top
             total[r] = total[r] * keep + jnp.sum(w0 + w1, axis=1, keepdims=True)
             w = jnp.concatenate([w0, w1], axis=1).astype(BF16)
-            term = dot(w, latent)
+            term = dot_t(w, keys[:LAT])
             for p in range(4):
                 lanes = slice(p * 128, (p + 1) * 128)
                 acc[r, :, lanes] = acc[r, :, lanes] * keep + term[:, lanes]
@@ -427,8 +416,8 @@
         scratch_shapes=[
             pltpu.VMEM(w_absorb.shape, BF16),
             pltpu.VMEM(w_value.shape, BF16),
-            pltpu.VMEM(cache.shape, BF16),
-            pltpu.VMEM(prefill_rows.shape[1:], BF16),
+            pltpu.VMEM((2, ROW, CTX), BF16),
+            pltpu.VMEM((8, ROW, BLK), BF16),
             pltpu.VMEM((8, KMSG, 128), BF16),
             pltpu.VMEM((8, KMSG, 128), BF16),
             pltpu.VMEM((2, NZ, NX, QMSG, 128), BF16),
@@ -463,11 +452,11 @@
         q_rope.reshape(rows, ROPE),
         w_absorb,
         w_value,
-        cache,
+        cache.transpose(0, 2, 1),
         res_len,
-        prefill_rows,
+        prefill_rows.transpose(0, 1, 3, 2),
         block_dest,
-        new_rows,
+        new_rows.transpose(1, 0, 2),
     )
     return out.reshape(q_nope.shape)
 

time: 66.6 us -> 55.6 us (0.83)
  local copies, waits for them, and re-layouts: 12.8 us -> 1.35 us
    unnamed x4 -> x1, local copies, waits for them, and re-layouts: 12.8 us -> 1.35 us
where the time goes in v2:
time: 55.6 us; the launch traced here: 55.1 us
  Pallas kernels  53.7 us (97%)
  local copies, waits for them, and re-layouts  1.35 us (2%)
    pallas_call x1, Pallas kernels, body(): pl.pallas_call(kernel, out_shape=jax.ShapeDtypeStruct((rows, 128), BF16),...  53.7 us
    unnamed x1, local copies, waits for them, and re-layouts  1.35 us

profile of v2, /device:TPU:0, one launch (start us, length us, event | category | flops | bytes accessed | tf_op | source)
XLA Modules:
  0.0 55.1 jit_solution(16728406415206094764)
XLA Ops:
  0.0 53.7 %latent_attention.1 = bf16[96,128]{1,0:T(8,128)(2,1)} custom-call(bf16[96,128]{1,0:T(8,128)(2,1)} %bitcast.9, bf16[96,64]{1,0:T(8,128)(2,1)} %bitcast.10, bf16[8,128,512]{2,1,0:T(8,128)(2,1)} %wa_hbm.1, bf16[8,512,128]{2,1,0:T(8,128)(2,1)} %wv_hbm.1, bf16[2,576,2048]{2,1,0:T(8,128)(2,1)} %bitcast.6, s32[2]{0:T(128)} %len_ref.1, ...), custom_call_target="tpu_custom_call" | custom-call | tf_op jit(solution)/shard_map/latent_attention/pallas_call | solution.py:411
  53.7 1.3 %copy.11 = bf16[4,3,8,128]{3,2,1,0:T(8,128)(2,1)} copy(bf16[4,3,8,128]{3,2,1,0:T(8,128)(2,1)} %bitcast.8) | data formatting | bytes 49152

commit v3 on v2

--- a/solution.py
+++ b/solution.py
@@ -29,7 +29,7 @@
 NEG = -1e30
 EXPC = (128 + 64) ** -0.5 * math.log2(math.e)
 
-GROUP = [(0, 0), (0, 1), (1, 0), (1, 1), (3, 0), (3, 1), (2, 0), (2, 1)]
+ALONG_Y = (1, 3, 2)
 
 
 def dot_t(a, b):
@@ -41,9 +41,9 @@
 
 
 def kernel(
-    qn_ref, qr_ref, wa_hbm, wv_hbm, cache_hbm, len_ref, pre_hbm, dest_ref, new_ref,
+    qn_hbm, qr_hbm, wa_hbm, wv_hbm, cache_hbm, len_hbm, pre_hbm, dest_hbm, new_hbm,
     out_ref,
-    wa, wv, cache, pre, ysend, kv, qbuf, qall, scores, weights, acc, peak, total,
+    qn_ref, qr_ref, len_ref, dest_ref, new_ref, wa, wv, cache, pre, ysend, kv, qbuf, qall, scores, weights, acc, peak, total,
     fresh, fresh_w, fresh_m, fresh_l, pout, pin,
     local_sem, y_ss, y_rs, a_ss, a_rs, f_ss, f_rs, p_ss, p_rs,
 ):
@@ -51,8 +51,8 @@
     y, c = lax.div(g, NC), lax.rem(g, NC)
     z, x = lax.div(s, NX), lax.rem(s, NX)
 
-    def group_of(dy, dc):
-        return lax.rem(y + dy, NY) * NC + lax.rem(c + dc, NC)
+    def group_dev(dy, core):
+        return (lax.rem(y + dy, NY) * NC + core, s)
 
     def seq_dev(dz, dx):
         return (g, lax.rem(z + dz, NZ) * NX + lax.rem(x + dx, NX))
@@ -60,27 +60,31 @@
     loads = [
         pltpu.make_async_copy(src, dst, local_sem.at[i])
         for i, (src, dst) in enumerate(
-            [(pre_hbm.at[0], pre), (wa_hbm, wa), (cache_hbm, cache), (wv_hbm, wv)]
+            [
+                (dest_hbm, dest_ref), (pre_hbm.at[0], pre), (qn_hbm, qn_ref), (qr_hbm, qr_ref), (wa_hbm, wa),
+                (new_hbm, new_ref), (len_hbm, len_ref), (cache_hbm, cache), (wv_hbm, wv),
+            ]
         )
     ]
-    for load in loads:
+    barrier = pltpu.get_barrier_semaphore()
+    for load in loads[:5]:
         load.start()
-
-    barrier = pltpu.get_barrier_semaphore()
-    for dy, dc in GROUP[1:]:
-        pl.semaphore_signal(barrier, inc=1, device_id=(group_of(dy, dc), s), device_id_type=MESH)
-    for j in range(1, NSEQ):
-        pl.semaphore_signal(
-            barrier, inc=1, device_id=seq_dev(j // NX, j % NX), device_id_type=MESH
-        )
-
+    for device in (
+        [group_dev(dy, core) for dy in ALONG_Y for core in range(NC)]
+        + [group_dev(0, 1 - c)]
+        + [seq_dev(j // NX, j % NX) for j in range(1, NSEQ)]
+    ):
+        pl.semaphore_signal(barrier, inc=1, device_id=device, device_id_type=MESH)
+    for load in loads[5:]:
+        load.start()
+
+    loads[0].wait()
     owners = [dest_ref[0, k] for k in range(8)]
     targets = [lax.div(o, 2) for o in owners]
     members = [lax.rem(o, 2) for o in owners]
-    loads[0].wait()
     tag_row = lax.broadcasted_iota(jnp.int32, (16, 128), 0)
-    for i, (dy, dc) in enumerate(GROUP):
-        wanted = group_of(dy, dc)
+
+    def pick(to, wanted):
         first = second = jnp.int32(0)
         tag_first = tag_second = jnp.int32(2)
         for k in reversed(range(8)):
@@ -89,13 +93,38 @@
             tag_second = jnp.where(match, tag_first, tag_second)
             first = jnp.where(match, k, first)
             tag_first = jnp.where(match, members[k], tag_first)
-        to = kv if i == 0 else ysend
         for slot, index in enumerate((first, second)):
-            to[i, pl.ds(slot * ROW, ROW), :] = pre[index]
+            to[pl.ds(slot * ROW, ROW), :] = pre[index]
         tags = jnp.where(tag_row < 8, tag_first, tag_second)
-        to[i, pl.ds(2 * ROW, 16), :] = tags.astype(F32).astype(BF16)
+        to[pl.ds(2 * ROW, 16), :] = tags.astype(F32).astype(BF16)
+
+    def core_copy():
+        return pltpu.make_async_remote_copy(
+            src_ref=ysend.at[6], dst_ref=kv.at[1], send_sem=y_ss.at[6], recv_sem=y_rs.at[1],
+            device_id=group_dev(0, 1 - c), device_id_type=MESH,
+        )
+
+    def y_copy(k, core):
+        there = 2 + 2 * ALONG_Y.index((NY - ALONG_Y[k]) % NY) + c
+        return pltpu.make_async_remote_copy(
+            src_ref=ysend.at[3 * core + k], dst_ref=kv.at[there],
+            send_sem=y_ss.at[3 * core + k], recv_sem=y_rs.at[there],
+            device_id=group_dev(ALONG_Y[k], core), device_id_type=MESH,
+        )
+
+    def blocks_to(core):
+        copies = [y_copy(k, core) for k in range(3)]
+        for k, copy in enumerate(copies):
+            pick(ysend.at[3 * core + k], lax.rem(y + ALONG_Y[k], NY) * NC + core)
+            copy.start()
+        return copies
 
     loads[1].wait()
+    pl.semaphore_wait(barrier, 7 + NSEQ - 1)
+    group_copies = blocks_to(0)
+
+    for load in loads[2:5]:
+        load.wait()
     row = lax.broadcasted_iota(jnp.int32, (2 * ROWS, 128), 0)
     own = qn_ref[...].astype(F32)
     spread = [jnp.where((row & 7) == h, own, 0.0).astype(BF16) for h in range(HEADS)]
@@ -108,20 +137,6 @@
             qbuf[pair, 0, 0, pl.ds(p * ROWS, ROWS), :] = q_latent[rows, p * 128 : (p + 1) * 128]
         qbuf[pair, 0, 0, pl.ds(4 * ROWS, ROWS), :] = q_rope[rows]
 
-    pl.semaphore_wait(barrier, 7 + NSEQ - 1)
-
-    def group_copy(i):
-        dy, dc = GROUP[i]
-        there = GROUP.index(((NY - dy) % NY, dc))
-        return pltpu.make_async_remote_copy(
-            src_ref=ysend.at[i], dst_ref=kv.at[there], send_sem=y_ss.at[i], recv_sem=y_rs.at[there],
-            device_id=(group_of(dy, dc), s), device_id_type=MESH,
-        )
-
-    group_copies = [group_copy(i) for i in range(1, 8)]
-    for copy in group_copies:
-        copy.start()
-
     low, high = pl.ds(0, QCUT), pl.ds(QCUT, QMSG - QCUT)
 
     def own_copy(pair, index, dz, dx, rows):
@@ -176,6 +191,12 @@
     others = start(rest(0))
     sent += first_x + first_z + others
 
+    group_copies += blocks_to(1)
+    pick(ysend.at[6], y * NC + 1 - c)
+    group_copies += start([core_copy()])
+    pick(kv.at[0], y * NC + c)
+
+    loads[5].wait()
     fresh[...] = jnp.zeros_like(fresh)
     for u in range(STEPS):
         new = new_ref[u].astype(F32)
@@ -318,7 +339,8 @@
 
     arrived(others + forward_z0 + forward_x0)
     assemble(0)
-    loads[2].wait()
+    loads[6].wait()
+    loads[7].wait()
 
     def resident(r, carry):
         limit = len_ref[r] - s * CTX
@@ -357,44 +379,50 @@
         total[r] = jnp.zeros((QROWS, 128), F32)
 
     def blocks(i):
-        keys = jnp.concatenate([kv[i, pl.ds(0, ROW), :], kv[i, pl.ds(ROW, ROW), :]], axis=1)
-        tags = kv[i, pl.ds(2 * ROW, 16), :].astype(F32)
-        tag = jnp.concatenate([tags[0:1, :], tags[8:9, :]], axis=1)
+        keys = jnp.concatenate(
+            [kv[i + n // 2, pl.ds(n % 2 * ROW, ROW), :] for n in range(4)], axis=1
+        )
+        tags = [kv[i + n, pl.ds(2 * ROW, 16), :].astype(F32) for n in range(2)]
+        tag = jnp.concatenate([tags[n // 2][n % 2 * 8 : n % 2 * 8 + 1, :] for n in range(4)], axis=1)
         for r in (2, 3):
             sc = dot(qall[r, :, :ROW], keys)
             sc = jnp.where(tag == float(r - 2), sc, NEG)
             old = peak[r]
-            best = jnp.max(
-                jnp.maximum(sc[:, :128], sc[:, 128:]), axis=1, keepdims=True
+            best = jnp.maximum(
+                jnp.maximum(sc[:, :128], sc[:, 128:256]), jnp.maximum(sc[:, 256:384], sc[:, 384:])
             )
-            top = jnp.maximum(old, best)
+            top = jnp.maximum(old, jnp.max(best, axis=1, keepdims=True))
             keep = jnp.exp2((old - top) * EXPC)
-            w0 = jnp.exp2((sc[:, :128] - top) * EXPC)
-            w1 = jnp.exp2((sc[:, 128:] - top) * EXPC)
+            w = [jnp.exp2((sc[:, n * 128 : (n + 1) * 128] - top) * EXPC) for n in range(4)]
             peak[r] = top
-            total[r] = total[r] * keep + jnp.sum(w0 + w1, axis=1, keepdims=True)
-            w = jnp.concatenate([w0, w1], axis=1).astype(BF16)
+            total[r] = total[r] * keep + jnp.sum((w[0] + w[1]) + (w[2] + w[3]), axis=1, keepdims=True)
+            w = jnp.concatenate(w, axis=1).astype(BF16)
             term = dot_t(w, keys[:LAT])
             for p in range(4):
                 lanes = slice(p * 128, (p + 1) * 128)
                 acc[r, :, lanes] = acc[r, :, lanes] * keep + term[:, lanes]
 
-    def landed(i, carry):
+    def landed(i):
         pltpu.make_async_remote_copy(
-            src_ref=ysend.at[i], dst_ref=kv.at[i], send_sem=y_ss.at[i], recv_sem=y_rs.at[i],
-            device_id=(group_of(0, 1), s), device_id_type=MESH,
+            src_ref=ysend.at[6], dst_ref=kv.at[i], send_sem=y_ss.at[6], recv_sem=y_rs.at[i],
+            device_id=group_dev(0, 1 - c), device_id_type=MESH,
         ).wait_recv()
-        blocks(i)
+
+    landed(1)
+    blocks(0)
+
+    def four(k, carry):
+        landed(2 * k)
+        landed(2 * k + 1)
+        blocks(2 * k)
         return carry
 
-    blocks(0)
-    lax.fori_loop(1, 6, landed, 0)
-    loads[3].wait()
+    lax.fori_loop(1, 4, four, 0)
+    pack(1)
+    partials1 = start(partial_copies(1))
+    loads[8].wait()
     arrived(partials0)
     finish(0)
-    lax.fori_loop(6, 8, landed, 0)
-    pack(1)
-    partials1 = start(partial_copies(1))
     arrived(partials1)
     finish(1)
     for copy in group_copies + sent + partials0 + partials1:
@@ -403,22 +431,22 @@
 
 def body(q_nope, q_rope, w_absorb, w_value, cache, res_len, prefill_rows, block_dest, new_rows):
     rows = 4 * PART
-    vmem, hbm, smem = (
-        pl.BlockSpec(memory_space=pltpu.VMEM),
-        pl.BlockSpec(memory_space=pl.ANY),
-        pl.BlockSpec(memory_space=pltpu.SMEM),
-    )
     out = pl.pallas_call(
         kernel,
         out_shape=jax.ShapeDtypeStruct((rows, 128), BF16),
-        in_specs=[vmem, vmem, hbm, hbm, hbm, smem, hbm, smem, vmem],
-        out_specs=vmem,
+        in_specs=[pl.BlockSpec(memory_space=pl.ANY)] * 9,
+        out_specs=pl.BlockSpec(memory_space=pltpu.VMEM),
         scratch_shapes=[
+            pltpu.VMEM((rows, 128), BF16),
+            pltpu.VMEM((rows, ROPE), BF16),
+            pltpu.SMEM(res_len.shape, jnp.int32),
+            pltpu.SMEM(block_dest.shape, jnp.int32),
+            pltpu.VMEM((STEPS, 4, ROW), BF16),
             pltpu.VMEM(w_absorb.shape, BF16),
             pltpu.VMEM(w_value.shape, BF16),
             pltpu.VMEM((2, ROW, CTX), BF16),
             pltpu.VMEM((8, ROW, BLK), BF16),
-            pltpu.VMEM((8, KMSG, 128), BF16),
+            pltpu.VMEM((7, KMSG, 128), BF16),
             pltpu.VMEM((8, KMSG, 128), BF16),
             pltpu.VMEM((2, NZ, NX, QMSG, 128), BF16),
             pltpu.VMEM((4, QROWS, LAT + 128), BF16),
@@ -433,8 +461,8 @@
             pltpu.VMEM((rows, 128), F32),
             pltpu.VMEM((2, NSEQ, PMSG, 128), BF16),
             pltpu.VMEM((2, NSEQ, PMSG, 128), BF16),
-            pltpu.SemaphoreType.DMA((4,)),
-            pltpu.SemaphoreType.DMA((8,)),
+            pltpu.SemaphoreType.DMA((9,)),
+            pltpu.SemaphoreType.DMA((7,)),
             pltpu.SemaphoreType.DMA((8,)),
             pltpu.SemaphoreType.DMA((2, 12)),
             pltpu.SemaphoreType.DMA((2, 12)),

time: 55.6 us -> 50.9 us (0.915)
  the two profiles are of different devices: /device:TPU:0 before, /device:TPU:1 now
where the time goes in v3:
time: 50.9 us; the launch traced here: 50.7 us
  Pallas kernels  49.4 us (97%)
  local copies, waits for them, and re-layouts  1.35 us (3%)
    pallas_call x1, Pallas kernels, body(): pl.pallas_call(kernel, out_shape=jax.ShapeDtypeStruct((rows, 128), BF16),...  49.4 us
    unnamed x1, local copies, waits for them, and re-layouts  1.35 us

profile of v3, /device:TPU:1, one launch (start us, length us, event | category | flops | bytes accessed | tf_op | source)
XLA Modules:
  0.0 50.7 jit_solution(9945312022924198876)
XLA Ops:
  0.0 49.4 %latent_attention.1 = bf16[96,128]{1,0:T(8,128)(2,1)} custom-call(bf16[96,128]{1,0:T(8,128)(2,1)} %bitcast.9, bf16[96,64]{1,0:T(8,128)(2,1)} %bitcast.10, bf16[8,128,512]{2,1,0:T(8,128)(2,1)} %wa_hbm.1, bf16[8,512,128]{2,1,0:T(8,128)(2,1)} %wv_hbm.1, bf16[2,576,2048]{2,1,0:T(8,128)(2,1)} %bitcast.6, s32[2]{0:T(128)} %len_hbm.1, ...), custom_call_target="tpu_custom_call" | custom-call | tf_op jit(solution)/shard_map/latent_attention/pallas_call | solution.py:434
  49.4 1.3 %copy.11 = bf16[4,3,8,128]{3,2,1,0:T(8,128)(2,1)} copy(bf16[4,3,8,128]{3,2,1,0:T(8,128)(2,1)} %bitcast.8) | data formatting | bytes 49152

commit v4 on v3

--- a/solution.py
+++ b/solution.py
@@ -1,3 +1,4 @@
+import functools
 import math
 
 import jax
@@ -21,15 +22,18 @@
 LAT, ROPE = 512, 64
 BLK = 128
 CTX = 2048
-QMSG = 5 * ROWS
-QCUT = 128
+QMSG = 4 * ROWS + 32
+QCUT = QMSG // 2
 PMSG = 4 * ROWS + 16
 ROW = LAT + ROPE
-KMSG = 2 * ROW + 16
+KMSG = 16 + 2 * ROW
 NEG = -1e30
 EXPC = (128 + 64) ** -0.5 * math.log2(math.e)
 
 ALONG_Y = (1, 3, 2)
+FAR_FIRST = [
+    (1, 2), (2, 1), (3, 2), (2, 3), (2, 2), (1, 1), (3, 3), (1, 3), (3, 1), (0, 2), (2, 0), (0, 1), (1, 0), (0, 3), (3, 0),
+]
 
 
 def dot_t(a, b):
@@ -75,8 +79,14 @@
         + [seq_dev(j // NX, j % NX) for j in range(1, NSEQ)]
     ):
         pl.semaphore_signal(barrier, inc=1, device_id=device, device_id_type=MESH)
+
     for load in loads[5:]:
         load.start()
+
+    def start(copies):
+        for copy in copies:
+            copy.start()
+        return copies
 
     loads[0].wait()
     owners = [dest_ref[0, k] for k in range(8)]
@@ -94,9 +104,9 @@
             first = jnp.where(match, k, first)
             tag_first = jnp.where(match, members[k], tag_first)
         for slot, index in enumerate((first, second)):
-            to[pl.ds(slot * ROW, ROW), :] = pre[index]
+            to[pl.ds(16 + slot * ROW, ROW), :] = pre[index]
         tags = jnp.where(tag_row < 8, tag_first, tag_second)
-        to[pl.ds(2 * ROW, 16), :] = tags.astype(F32).astype(BF16)
+        to[pl.ds(0, 16), :] = tags.astype(F32).astype(BF16)
 
     def core_copy():
         return pltpu.make_async_remote_copy(
@@ -104,23 +114,27 @@
             device_id=group_dev(0, 1 - c), device_id_type=MESH,
         )
 
-    def y_copy(k, core):
+    parts = [pl.ds(0, KMSG), pl.ds(0, 16 + ROW), pl.ds(16 + ROW, ROW)]
+
+    def y_copy(k, core, part):
         there = 2 + 2 * ALONG_Y.index((NY - ALONG_Y[k]) % NY) + c
+        late = 2 if part == 2 else 0
         return pltpu.make_async_remote_copy(
-            src_ref=ysend.at[3 * core + k], dst_ref=kv.at[there],
-            send_sem=y_ss.at[3 * core + k], recv_sem=y_rs.at[there],
+            src_ref=ysend.at[3 * core + k, parts[part]], dst_ref=kv.at[there, parts[part]],
+            send_sem=y_ss.at[3 * core + k + (5 - 2 * core if late else 0)], recv_sem=y_rs.at[there + late],
             device_id=group_dev(ALONG_Y[k], core), device_id_type=MESH,
         )
 
     def blocks_to(core):
-        copies = [y_copy(k, core) for k in range(3)]
-        for k, copy in enumerate(copies):
+        copies = []
+        for k in range(3):
             pick(ysend.at[3 * core + k], lax.rem(y + ALONG_Y[k], NY) * NC + core)
-            copy.start()
+            copies += start([y_copy(k, core, part) for part in ((0,) if k < 2 else (1, 2))])
         return copies
 
     loads[1].wait()
-    pl.semaphore_wait(barrier, 7 + NSEQ - 1)
+    pl.semaphore_wait(barrier, 2 * NY - 1 + NSEQ - 1)
+
     group_copies = blocks_to(0)
 
     for load in loads[2:5]:
@@ -130,12 +144,16 @@
     spread = [jnp.where((row & 7) == h, own, 0.0).astype(BF16) for h in range(HEADS)]
     q_latent = dot(jnp.concatenate(spread, axis=1), wa[...].reshape(HEADS * 128, LAT))
     q_latent = q_latent.astype(BF16)
-    q_rope = jnp.concatenate([qr_ref[...], jnp.zeros((2 * ROWS, 128 - ROPE), BF16)], axis=1)
     for pair in range(2):
         rows = slice(pair * ROWS, (pair + 1) * ROWS)
         for p in range(4):
             qbuf[pair, 0, 0, pl.ds(p * ROWS, ROWS), :] = q_latent[rows, p * 128 : (p + 1) * 128]
-        qbuf[pair, 0, 0, pl.ds(4 * ROWS, ROWS), :] = q_rope[rows]
+        ropes = [qr_ref[pl.ds(pair * ROWS + 16 * i, 16), :] for i in range(3)]
+        ropes.append(jnp.zeros((16, ROPE), BF16))
+        for i in range(2):
+            qbuf[pair, 0, 0, pl.ds(4 * ROWS + 16 * i, 16), :] = jnp.concatenate(
+                ropes[2 * i : 2 * i + 2], axis=1
+            )
 
     low, high = pl.ds(0, QCUT), pl.ds(QCUT, QMSG - QCUT)
 
@@ -176,11 +194,6 @@
             )
             for d in (1, 2, 3)
         ]
-
-    def start(copies):
-        for copy in copies:
-            copy.start()
-        return copies
 
     def arrived(copies):
         for copy in copies:
@@ -236,9 +249,16 @@
         def two(i, carry):
             at = pl.multiple_of(i * 2 * PART, 16)
             dz, dx = lax.div(i, 2), lax.rem(i, 2) * 2
+            def part(d, p):
+                if p < 4:
+                    return qbuf[pair, dz, dx + d, pl.ds(p * ROWS, ROWS), :].astype(F32)
+                first, second = (
+                    qbuf[pair, dz, dx + d, pl.ds(4 * ROWS + 16 * i, 16), :].astype(F32) for i in range(2)
+                )
+                return jnp.concatenate([first, pltpu.roll(first, ROPE, 1), second], axis=0)
+
             for p in range(5):
-                one = qbuf[pair, dz, dx, pl.ds(p * ROWS, ROWS), :].astype(F32)
-                two = qbuf[pair, dz, dx + 1, pl.ds(p * ROWS, ROWS), :].astype(F32)
+                one, two = part(0, p), part(1, p)
                 lanes = slice(p * 128, (p + 1) * 128)
                 for r in range(2):
                     rows = slice(r * PART, (r + 1) * PART)
@@ -281,15 +301,17 @@
 
         lax.fori_loop(0, NSEQ, one, 0)
 
+    def partial_copy(pair, j):
+        dz, dx = lax.div(j, NX), lax.rem(j, NX)
+        there = lax.rem(NZ - dz, NZ) * NX + lax.rem(NX - dx, NX)
+        return pltpu.make_async_remote_copy(
+            src_ref=pout.at[pair, j], dst_ref=pin.at[pair, there],
+            send_sem=p_ss.at[pair, j], recv_sem=p_rs.at[pair, there],
+            device_id=seq_dev(dz, dx), device_id_type=MESH,
+        )
+
     def partial_copies(pair):
-        return [
-            pltpu.make_async_remote_copy(
-                src_ref=pout.at[pair, j], dst_ref=pin.at[pair, (NZ - j // NX) % NZ * NX + (NX - j % NX) % NX],
-                send_sem=p_ss.at[pair, j], recv_sem=p_rs.at[pair, j],
-                device_id=seq_dev(j // NX, j % NX), device_id_type=MESH,
-            )
-            for j in range(1, NSEQ)
-        ]
+        return [partial_copy(pair, dz * NX + dx) for dz, dx in FAR_FIRST]
 
     def finish(pair):
         stats = jnp.concatenate(
@@ -342,32 +364,47 @@
     loads[6].wait()
     loads[7].wait()
 
-    def resident(r, carry):
-        limit = len_ref[r] - s * CTX
-        tile = 512
-        position = lax.broadcasted_iota(jnp.int32, (QROWS, tile), 1)
-        running = jnp.full((QROWS, 128), NEG, F32)
-        for k in range(CTX // tile):
-            keys = pl.ds(k * tile, tile)
-            sc = dot(qall[r, :, :ROW], cache[r, :, keys])
-            sc = jnp.where(position < limit - k * tile, sc, NEG)
-            scores[:, keys] = sc
-            for i in range(tile // 128):
-                running = jnp.maximum(running, sc[:, i * 128 : (i + 1) * 128])
-        m = jnp.max(running, axis=1, keepdims=True)
-        sums = jnp.zeros((QROWS, 128), F32)
-        for k in range(CTX // tile):
-            keys = pl.ds(k * tile, tile)
-            w = jnp.exp2((scores[:, keys] - m) * EXPC)
-            for i in range(tile // 128):
-                sums = sums + w[:, i * 128 : (i + 1) * 128]
-            weights[:, keys] = w.astype(BF16)
-        acc[r] = dot_t(weights[...], cache[r, :LAT, :])
+    tile = 512
+    tiles = range(CTX // tile)
+    position = lax.broadcasted_iota(jnp.int32, (QROWS, tile), 1)
+
+    def score(r, k, running):
+        keys = pl.ds(k * tile, tile)
+        sc = dot(qall[r, :, :ROW], cache[r, :, keys])
+        sc = jnp.where(position < len_ref[r] - s * CTX - k * tile, sc, NEG)
+        scores[r, :, keys] = sc
+        for i in range(tile // 128):
+            running = jnp.maximum(running, sc[:, i * 128 : (i + 1) * 128])
+        return running
+
+    def weigh(r, k, m, sums):
+        keys = pl.ds(k * tile, tile)
+        w = jnp.exp2((scores[r, :, keys] - m) * EXPC)
+        for i in range(tile // 128):
+            sums = sums + w[:, i * 128 : (i + 1) * 128]
+        weights[r, :, keys] = w.astype(BF16)
+        return sums
+
+    def done(r, m, sums):
         peak[r] = jnp.broadcast_to(m, (QROWS, 128))
         total[r] = jnp.broadcast_to(jnp.sum(sums, axis=1, keepdims=True), (QROWS, 128))
-        return carry
-
-    lax.fori_loop(0, 2, resident, 0)
+
+    lowest, nothing = jnp.full((QROWS, 128), NEG, F32), jnp.zeros((QROWS, 128), F32)
+    m0 = m1 = lowest
+    for k in tiles:
+        m0 = score(0, k, m0)
+    m0 = jnp.max(m0, axis=1, keepdims=True)
+    sums0 = sums1 = nothing
+    for k in tiles:
+        m1 = score(1, k, m1)
+        sums0 = weigh(0, k, m0, sums0)
+    m1 = jnp.max(m1, axis=1, keepdims=True)
+    done(0, m0, sums0)
+    acc[0] = dot_t(weights[0], cache[0, :LAT, :])
+    for k in tiles:
+        sums1 = weigh(1, k, m1, sums1)
+    done(1, m1, sums1)
+    acc[1] = dot_t(weights[1], cache[1, :LAT, :])
     pack(0)
     partials0 = start(partial_copies(0))
 
@@ -378,46 +415,54 @@
         peak[r] = jnp.full((QROWS, 128), NEG, F32)
         total[r] = jnp.zeros((QROWS, 128), F32)
 
-    def blocks(i):
-        keys = jnp.concatenate(
-            [kv[i + n // 2, pl.ds(n % 2 * ROW, ROW), :] for n in range(4)], axis=1
-        )
-        tags = [kv[i + n, pl.ds(2 * ROW, 16), :].astype(F32) for n in range(2)]
-        tag = jnp.concatenate([tags[n // 2][n % 2 * 8 : n % 2 * 8 + 1, :] for n in range(4)], axis=1)
-        for r in (2, 3):
-            sc = dot(qall[r, :, :ROW], keys)
-            sc = jnp.where(tag == float(r - 2), sc, NEG)
-            old = peak[r]
-            best = jnp.maximum(
-                jnp.maximum(sc[:, :128], sc[:, 128:256]), jnp.maximum(sc[:, 256:384], sc[:, 384:])
-            )
-            top = jnp.maximum(old, jnp.max(best, axis=1, keepdims=True))
+    def blocks(taken):
+        keys = jnp.concatenate([kv[i, pl.ds(16 + slot * ROW, ROW), :] for i, slot in taken], axis=1)
+        tag = jnp.concatenate(
+            [kv[i, pl.ds(0, 16), :].astype(F32)[8 * slot : 8 * slot + 1] for i, slot in taken], axis=1
+        )
+        count = len(taken)
+        new = (2, 3)
+        scs = [jnp.where(tag == float(r - 2), dot(qall[r, :, :ROW], keys), NEG) for r in new]
+        pieces = [[sc[:, n * 128 : (n + 1) * 128] for n in range(count)] for sc in scs]
+        olds = [peak[r] for r in new]
+        tops = [
+            jnp.maximum(old, jnp.max(functools.reduce(jnp.maximum, some), axis=1, keepdims=True))
+            for old, some in zip(olds, pieces)
+        ]
+        ws = [[jnp.exp2((piece - top) * EXPC) for piece in some] for some, top in zip(pieces, tops)]
+        terms = [dot_t(jnp.concatenate(w, axis=1).astype(BF16), keys[:LAT]) for w in ws]
+        for r, old, top, w, term in zip(new, olds, tops, ws, terms):
             keep = jnp.exp2((old - top) * EXPC)
-            w = [jnp.exp2((sc[:, n * 128 : (n + 1) * 128] - top) * EXPC) for n in range(4)]
             peak[r] = top
-            total[r] = total[r] * keep + jnp.sum((w[0] + w[1]) + (w[2] + w[3]), axis=1, keepdims=True)
-            w = jnp.concatenate(w, axis=1).astype(BF16)
-            term = dot_t(w, keys[:LAT])
+            total[r] = total[r] * keep + jnp.sum(sum(w[1:], w[0]), axis=1, keepdims=True)
             for p in range(4):
                 lanes = slice(p * 128, (p + 1) * 128)
                 acc[r, :, lanes] = acc[r, :, lanes] * keep + term[:, lanes]
 
-    def landed(i):
+    def landed(i, part, sem):
         pltpu.make_async_remote_copy(
-            src_ref=ysend.at[6], dst_ref=kv.at[i], send_sem=y_ss.at[6], recv_sem=y_rs.at[i],
+            src_ref=ysend.at[6, parts[part]], dst_ref=kv.at[i, parts[part]],
+            send_sem=y_ss.at[6], recv_sem=y_rs.at[sem],
             device_id=group_dev(0, 1 - c), device_id_type=MESH,
         ).wait_recv()
 
-    landed(1)
-    blocks(0)
+    landed(1, 0, 1)
 
     def four(k, carry):
-        landed(2 * k)
-        landed(2 * k + 1)
-        blocks(2 * k)
+        @pl.when(k > 0)
+        def _():
+            landed(2 * k, 0, 2 * k)
+            landed(2 * k + 1, 0, 2 * k + 1)
+
+        blocks([(2 * k, 0), (2 * k, 1), (2 * k + 1, 0), (2 * k + 1, 1)])
         return carry
 
-    lax.fori_loop(1, 4, four, 0)
+    lax.fori_loop(0, 3, four, 0)
+    landed(6, 1, 6)
+    landed(7, 1, 7)
+    landed(6, 2, 8)
+    landed(7, 2, 9)
+    blocks([(6, 0), (6, 1), (7, 0), (7, 1)])
     pack(1)
     partials1 = start(partial_copies(1))
     loads[8].wait()
@@ -450,8 +495,8 @@
             pltpu.VMEM((8, KMSG, 128), BF16),
             pltpu.VMEM((2, NZ, NX, QMSG, 128), BF16),
             pltpu.VMEM((4, QROWS, LAT + 128), BF16),
-            pltpu.VMEM((QROWS, CTX), F32),
-            pltpu.VMEM((QROWS, CTX), BF16),
+            pltpu.VMEM((2, QROWS, CTX), F32),
+            pltpu.VMEM((2, QROWS, CTX), BF16),
             pltpu.VMEM((4, QROWS, LAT), F32),
             pltpu.VMEM((4, QROWS, 128), F32),
             pltpu.VMEM((4, QROWS, 128), F32),
@@ -462,8 +507,8 @@
             pltpu.VMEM((2, NSEQ, PMSG, 128), BF16),
             pltpu.VMEM((2, NSEQ, PMSG, 128), BF16),
             pltpu.SemaphoreType.DMA((9,)),
-            pltpu.SemaphoreType.DMA((7,)),
-            pltpu.SemaphoreType.DMA((8,)),
+            pltpu.SemaphoreType.DMA((9,)),
+            pltpu.SemaphoreType.DMA((10,)),
             pltpu.SemaphoreType.DMA((2, 12)),
             pltpu.SemaphoreType.DMA((2, 12)),
             pltpu.SemaphoreType.DMA((2, 6)),

time: 50.9 us -> 49.4 us (0.971)
  Pallas kernels: 49.4 us -> 47.8 us
    pallas_call x1, Pallas kernels: 49.4 us -> 47.8 us  [body(): pl.pallas_call(kernel, out_shape=jax.ShapeDtypeStruct((rows, 128), BF16),...]
where the time goes in v4:
time: 49.4 us; the launch traced here: 49.2 us
  Pallas kernels  47.8 us (97%)
  local copies, waits for them, and re-layouts  1.35 us (3%)
    pallas_call x1, Pallas kernels, body(): pl.pallas_call(kernel, out_shape=jax.ShapeDtypeStruct((rows, 128), BF16),...  47.8 us
    unnamed x1, local copies, waits for them, and re-layouts  1.35 us

profile of v4, /device:TPU:1, one launch (start us, length us, event | category | flops | bytes accessed | tf_op | source)
XLA Modules:
  0.0 49.2 jit_solution(17326331175815550482)
XLA Ops:
  0.0 47.8 %latent_attention.1 = bf16[96,128]{1,0:T(8,128)(2,1)} custom-call(bf16[96,128]{1,0:T(8,128)(2,1)} %bitcast.9, bf16[96,64]{1,0:T(8,128)(2,1)} %bitcast.10, bf16[8,128,512]{2,1,0:T(8,128)(2,1)} %wa_hbm.1, bf16[8,512,128]{2,1,0:T(8,128)(2,1)} %wv_hbm.1, bf16[2,576,2048]{2,1,0:T(8,128)(2,1)} %bitcast.6, s32[2]{0:T(128)} %len_hbm.1, ...), custom_call_target="tpu_custom_call" | custom-call | tf_op jit(solution)/shard_map/latent_attention/pallas_call | solution.py:479
  47.8 1.3 %copy.11 = bf16[4,3,8,128]{3,2,1,0:T(8,128)(2,1)} copy(bf16[4,3,8,128]{3,2,1,0:T(8,128)(2,1)} %bitcast.8) | data formatting | bytes 49152

commit v5 on v4

--- a/solution.py
+++ b/solution.py
@@ -71,16 +71,15 @@
         )
     ]
     barrier = pltpu.get_barrier_semaphore()
-    for load in loads[:5]:
-        load.start()
     for device in (
         [group_dev(dy, core) for dy in ALONG_Y for core in range(NC)]
         + [group_dev(0, 1 - c)]
-        + [seq_dev(j // NX, j % NX) for j in range(1, NSEQ)]
+        + [seq_dev(0, d) for d in (1, 2, 3)]
+        + [seq_dev(d, 0) for d in (1, 2, 3)]
     ):
         pl.semaphore_signal(barrier, inc=1, device_id=device, device_id_type=MESH)
 
-    for load in loads[5:]:
+    for load in loads:
         load.start()
 
     def start(copies):
@@ -125,17 +124,17 @@
             device_id=group_dev(ALONG_Y[k], core), device_id_type=MESH,
         )
 
-    def blocks_to(core):
-        copies = []
+    def pick_for(core):
         for k in range(3):
             pick(ysend.at[3 * core + k], lax.rem(y + ALONG_Y[k], NY) * NC + core)
-            copies += start([y_copy(k, core, part) for part in ((0,) if k < 2 else (1, 2))])
-        return copies
+
+    def blocks_to(core):
+        return start(
+            [y_copy(k, core, part) for k in range(3) for part in (0,)]
+        )
 
     loads[1].wait()
-    pl.semaphore_wait(barrier, 2 * NY - 1 + NSEQ - 1)
-
-    group_copies = blocks_to(0)
+    pick_for(0)
 
     for load in loads[2:5]:
         load.wait()
@@ -155,6 +154,9 @@
                 ropes[2 * i : 2 * i + 2], axis=1
             )
 
+    pl.semaphore_wait(barrier, 2 * NY - 1 + 6)
+    group_copies = blocks_to(0)
+
     low, high = pl.ds(0, QCUT), pl.ds(QCUT, QMSG - QCUT)
 
     def own_copy(pair, index, dz, dx, rows):
@@ -199,11 +201,22 @@
         for copy in copies:
             copy.wait_recv()
 
-    sent = []
     first_x, first_z = start(x_first(0)), start(z_first(0))
     others = start(rest(0))
-    sent += first_x + first_z + others
-
+    first_x1, first_z1 = start(x_first(1)), start(z_first(1))
+    arrived(first_x)
+    forward_z0 = start(forward_z(0))
+    arrived(first_z)
+    forward_x0 = start(forward_x(0))
+    others1 = start(rest(1))
+    sent = first_x + first_z + others + first_x1 + first_z1 + others1
+    arrived(first_x1)
+    forward_z1 = start(forward_z(1))
+    arrived(first_z1)
+    forward_x1 = start(forward_x(1))
+    sent += forward_z0 + forward_x0 + forward_z1 + forward_x1
+
+    pick_for(1)
     group_copies += blocks_to(1)
     pick(ysend.at[6], y * NC + 1 - c)
     group_copies += start([core_copy()])
@@ -233,18 +246,6 @@
     fresh_l[...] = jnp.broadcast_to(jnp.sum(p_fresh, axis=1, keepdims=True), fresh_l.shape)
     fresh_w[...] = dot(p_fresh.astype(BF16), fresh_rows[:, :LAT])
 
-    arrived(first_x)
-    sent += (forward_z0 := start(forward_z(0)))
-    arrived(first_z)
-    sent += (forward_x0 := start(forward_x(0)))
-    first_x1, first_z1 = start(x_first(1)), start(z_first(1))
-    others1 = start(rest(1))
-    sent += first_x1 + first_z1 + others1
-    arrived(first_x1)
-    sent += (forward_z1 := start(forward_z(1)))
-    arrived(first_z1)
-    sent += (forward_x1 := start(forward_x(1)))
-
     def assemble(pair):
         def two(i, carry):
             at = pl.multiple_of(i * 2 * PART, 16)
@@ -457,12 +458,7 @@
         blocks([(2 * k, 0), (2 * k, 1), (2 * k + 1, 0), (2 * k + 1, 1)])
         return carry
 
-    lax.fori_loop(0, 3, four, 0)
-    landed(6, 1, 6)
-    landed(7, 1, 7)
-    landed(6, 2, 8)
-    landed(7, 2, 9)
-    blocks([(6, 0), (6, 1), (7, 0), (7, 1)])
+    lax.fori_loop(0, 4, four, 0)
     pack(1)
     partials1 = start(partial_copies(1))
     loads[8].wait()

time: 49.4 us -> 48.7 us (0.986)
  Pallas kernels: 47.8 us -> 47.2 us
    pallas_call x1, Pallas kernels: 47.8 us -> 47.2 us  [body(): pl.pallas_call(kernel, out_shape=jax.ShapeDtypeStruct((rows, 128), BF16),...]
where the time goes in v5:
time: 48.7 us; the launch traced here: 48.6 us
  Pallas kernels  47.2 us (97%)
  local copies, waits for them, and re-layouts  1.35 us (3%)
    pallas_call x1, Pallas kernels, body(): pl.pallas_call(kernel, out_shape=jax.ShapeDtypeStruct((rows, 128), BF16),...  47.2 us
    unnamed x1, local copies, waits for them, and re-layouts  1.35 us

profile of v5, /device:TPU:1, one launch (start us, length us, event | category | flops | bytes accessed | tf_op | source)
XLA Modules:
  0.0 48.6 jit_solution(5584677588399463812)
XLA Ops:
  0.0 47.2 %latent_attention.1 = bf16[96,128]{1,0:T(8,128)(2,1)} custom-call(bf16[96,128]{1,0:T(8,128)(2,1)} %bitcast.9, bf16[96,64]{1,0:T(8,128)(2,1)} %bitcast.10, bf16[8,128,512]{2,1,0:T(8,128)(2,1)} %wa_hbm.1, bf16[8,512,128]{2,1,0:T(8,128)(2,1)} %wv_hbm.1, bf16[2,576,2048]{2,1,0:T(8,128)(2,1)} %bitcast.6, s32[2]{0:T(128)} %len_hbm.1, ...), custom_call_target="tpu_custom_call" | custom-call | tf_op jit(solution)/shard_map/latent_attention/pallas_call | solution.py:475
  47.2 1.3 %copy.11 = bf16[4,3,8,128]{3,2,1,0:T(8,128)(2,1)} copy(bf16[4,3,8,128]{3,2,1,0:T(8,128)(2,1)} %bitcast.8) | data formatting | bytes 49152

commit v6 on v5

--- a/solution.py
+++ b/solution.py
@@ -134,7 +134,10 @@
         )
 
     loads[1].wait()
-    pick_for(0)
+    pick_for(1)
+
+    pl.semaphore_wait(barrier, 2 * NY - 1 + 6)
+    group_copies = blocks_to(1)
 
     for load in loads[2:5]:
         load.wait()
@@ -154,9 +157,6 @@
                 ropes[2 * i : 2 * i + 2], axis=1
             )
 
-    pl.semaphore_wait(barrier, 2 * NY - 1 + 6)
-    group_copies = blocks_to(0)
-
     low, high = pl.ds(0, QCUT), pl.ds(QCUT, QMSG - QCUT)
 
     def own_copy(pair, index, dz, dx, rows):
@@ -216,8 +216,8 @@
     forward_x1 = start(forward_x(1))
     sent += forward_z0 + forward_x0 + forward_z1 + forward_x1
 
-    pick_for(1)
-    group_copies += blocks_to(1)
+    pick_for(0)
+    group_copies += blocks_to(0)
     pick(ysend.at[6], y * NC + 1 - c)
     group_copies += start([core_copy()])
     pick(kv.at[0], y * NC + c)
@@ -270,34 +270,32 @@
 
         lax.fori_loop(0, NSEQ // 2, two, 0)
 
+    def message(pair, j, lane, sums, peaks, totals):
+        for p in range(4):
+            lanes = slice(p * 128, (p + 1) * 128)
+            pout[pair, j, pl.ds(p * ROWS, ROWS), :] = jnp.concatenate(
+                [part[:, lanes] for part in sums], axis=0
+            ).astype(BF16)
+        m, l = jnp.concatenate(peaks, axis=0), jnp.concatenate(totals, axis=0)
+        m_high = m.astype(BF16).astype(F32)
+        m_mid = (m - m_high).astype(BF16).astype(F32)
+        m_low = m - m_high - m_mid
+        l_high = l.astype(BF16).astype(F32)
+        stats = jnp.zeros((16, 128), F32)
+        for i in range(3):
+            rows = slice(16 * i, 16 * (i + 1))
+            for q, value in enumerate((m_high, m_mid, m_low, l_high, l - l_high)):
+                stats = jnp.where(lane == 8 * i + q, value[rows], stats)
+        pout[pair, j, pl.ds(4 * ROWS, 16), :] = stats.astype(BF16)
+
     def pack(pair):
         lane = lax.broadcasted_iota(jnp.int32, (16, 128), 1)
 
         def one(j, carry):
-            at = pl.multiple_of(j * PART, 8)
-
-            def both(ref):
-                return jnp.concatenate(
-                    [ref[2 * pair, pl.ds(at, PART), :], ref[2 * pair + 1, pl.ds(at, PART), :]], axis=0
-                )
-
-            for p in range(4):
-                lanes = slice(p * 128, (p + 1) * 128)
-                pout[pair, j, pl.ds(p * ROWS, ROWS), :] = jnp.concatenate(
-                    [acc[2 * pair, pl.ds(at, PART), lanes], acc[2 * pair + 1, pl.ds(at, PART), lanes]],
-                    axis=0,
-                ).astype(BF16)
-            m, l = both(peak), both(total)
-            m_high = m.astype(BF16).astype(F32)
-            m_mid = (m - m_high).astype(BF16).astype(F32)
-            m_low = m - m_high - m_mid
-            l_high = l.astype(BF16).astype(F32)
-            stats = jnp.zeros((16, 128), F32)
-            for i in range(3):
-                rows = slice(16 * i, 16 * (i + 1))
-                for q, value in enumerate((m_high, m_mid, m_low, l_high, l - l_high)):
-                    stats = jnp.where(lane == 8 * i + q, value[rows], stats)
-            pout[pair, j, pl.ds(4 * ROWS, 16), :] = stats.astype(BF16)
+            rows = pl.ds(pl.multiple_of(j * PART, 8), PART)
+            message(
+                pair, j, lane, *([ref[2 * pair + r, rows, :] for r in range(2)] for ref in (acc, peak, total))
+            )
             return carry
 
         lax.fori_loop(0, NSEQ, one, 0)
@@ -416,7 +414,7 @@
         peak[r] = jnp.full((QROWS, 128), NEG, F32)
         total[r] = jnp.zeros((QROWS, 128), F32)
 
-    def blocks(taken):
+    def blocks(taken, last=False):
         keys = jnp.concatenate([kv[i, pl.ds(16 + slot * ROW, ROW), :] for i, slot in taken], axis=1)
         tag = jnp.concatenate(
             [kv[i, pl.ds(0, 16), :].astype(F32)[8 * slot : 8 * slot + 1] for i, slot in taken], axis=1
@@ -432,12 +430,31 @@
         ]
         ws = [[jnp.exp2((piece - top) * EXPC) for piece in some] for some, top in zip(pieces, tops)]
         terms = [dot_t(jnp.concatenate(w, axis=1).astype(BF16), keys[:LAT]) for w in ws]
-        for r, old, top, w, term in zip(new, olds, tops, ws, terms):
-            keep = jnp.exp2((old - top) * EXPC)
+        keeps = [jnp.exp2((old - top) * EXPC) for old, top in zip(olds, tops)]
+        totals = [
+            total[r] * keep + jnp.sum(sum(w[1:], w[0]), axis=1, keepdims=True)
+            for r, keep, w in zip(new, keeps, ws)
+        ]
+        four = [slice(p * 128, (p + 1) * 128) for p in range(4)]
+        if last:
+            lane = lax.broadcasted_iota(jnp.int32, (16, 128), 1)
+            for dz, dx in FAR_FIRST + [(0, 0)]:
+                j = dz * NX + dx
+                rows = slice(j * PART, (j + 1) * PART)
+                sums = [
+                    jnp.concatenate(
+                        [acc[r, rows, lanes] * keep[rows] + term[rows, lanes] for lanes in four], axis=1
+                    )
+                    for r, keep, term in zip(new, keeps, terms)
+                ]
+                message(1, j, lane, sums, [top[rows] for top in tops], [t[rows] for t in totals])
+                if j > 0:
+                    partial_copy(1, j).start()
+            return
+        for r, keep, top, sums, term in zip(new, keeps, tops, totals, terms):
             peak[r] = top
-            total[r] = total[r] * keep + jnp.sum(sum(w[1:], w[0]), axis=1, keepdims=True)
-            for p in range(4):
-                lanes = slice(p * 128, (p + 1) * 128)
+            total[r] = sums
+            for lanes in four:
                 acc[r, :, lanes] = acc[r, :, lanes] * keep + term[:, lanes]
 
     def landed(i, part, sem):
@@ -458,9 +475,11 @@
         blocks([(2 * k, 0), (2 * k, 1), (2 * k + 1, 0), (2 * k + 1, 1)])
         return carry
 
-    lax.fori_loop(0, 4, four, 0)
-    pack(1)
-    partials1 = start(partial_copies(1))
+    lax.fori_loop(0, 3, four, 0)
+    landed(6, 0, 6)
+    landed(7, 0, 7)
+    blocks([(6, 0), (6, 1), (7, 0), (7, 1)], last=True)
+    partials1 = partial_copies(1)
     loads[8].wait()
     arrived(partials0)
     finish(0)

time: 48.7 us -> 48.1 us (0.988)
  the two profiles are of different devices: /device:TPU:1 before, /device:TPU:0 now
where the time goes in v6:
time: 48.1 us; the launch traced here: 48 us
  Pallas kernels  46.6 us (97%)
  local copies, waits for them, and re-layouts  1.35 us (3%)
    pallas_call x1, Pallas kernels, body(): pl.pallas_call(kernel, out_shape=jax.ShapeDtypeStruct((rows, 128), BF16),...  46.6 us
    unnamed x1, local copies, waits for them, and re-layouts  1.35 us

profile of v6, /device:TPU:0, one launch (start us, length us, event | category | flops | bytes accessed | tf_op | source)
XLA Modules:
  0.0 48.0 jit_solution(13649725264062007633)
XLA Ops:
  0.0 46.6 %latent_attention.1 = bf16[96,128]{1,0:T(8,128)(2,1)} custom-call(bf16[96,128]{1,0:T(8,128)(2,1)} %bitcast.9, bf16[96,64]{1,0:T(8,128)(2,1)} %bitcast.10, bf16[8,128,512]{2,1,0:T(8,128)(2,1)} %wa_hbm.1, bf16[8,512,128]{2,1,0:T(8,128)(2,1)} %wv_hbm.1, bf16[2,576,2048]{2,1,0:T(8,128)(2,1)} %bitcast.6, s32[2]{0:T(128)} %len_hbm.1, ...), custom_call_target="tpu_custom_call" | custom-call | tf_op jit(solution)/shard_map/latent_attention/pallas_call | solution.py:494
  46.6 1.3 %copy.11 = bf16[4,3,8,128]{3,2,1,0:T(8,128)(2,1)} copy(bf16[4,3,8,128]{3,2,1,0:T(8,128)(2,1)} %bitcast.8) | data formatting | bytes 49152

commit v7 on v6

--- a/solution.py
+++ b/solution.py
@@ -270,6 +270,15 @@
 
         lax.fori_loop(0, NSEQ // 2, two, 0)
 
+    def partial_copy(pair, j):
+        dz, dx = lax.div(j, NX), lax.rem(j, NX)
+        there = lax.rem(NZ - dz, NZ) * NX + lax.rem(NX - dx, NX)
+        return pltpu.make_async_remote_copy(
+            src_ref=pout.at[pair, j], dst_ref=pin.at[pair, there],
+            send_sem=p_ss.at[pair, j], recv_sem=p_rs.at[pair, there],
+            device_id=seq_dev(dz, dx), device_id_type=MESH,
+        )
+
     def message(pair, j, lane, sums, peaks, totals):
         for p in range(4):
             lanes = slice(p * 128, (p + 1) * 128)
@@ -292,22 +301,16 @@
         lane = lax.broadcasted_iota(jnp.int32, (16, 128), 1)
 
         def one(j, carry):
-            rows = pl.ds(pl.multiple_of(j * PART, 8), PART)
+            rows = pl.ds(j * PART, PART)
             message(
                 pair, j, lane, *([ref[2 * pair + r, rows, :] for r in range(2)] for ref in (acc, peak, total))
             )
             return carry
 
-        lax.fori_loop(0, NSEQ, one, 0)
-
-    def partial_copy(pair, j):
-        dz, dx = lax.div(j, NX), lax.rem(j, NX)
-        there = lax.rem(NZ - dz, NZ) * NX + lax.rem(NX - dx, NX)
-        return pltpu.make_async_remote_copy(
-            src_ref=pout.at[pair, j], dst_ref=pin.at[pair, there],
-            send_sem=p_ss.at[pair, j], recv_sem=p_rs.at[pair, there],
-            device_id=seq_dev(dz, dx), device_id_type=MESH,
-        )
+        for dz, dx in FAR_FIRST + [(0, 0)]:
+            one(dz * NX + dx, 0)
+            if dz or dx:
+                partial_copy(pair, dz * NX + dx).start()
 
     def partial_copies(pair):
         return [partial_copy(pair, dz * NX + dx) for dz, dx in FAR_FIRST]
@@ -405,7 +408,7 @@
     done(1, m1, sums1)
     acc[1] = dot_t(weights[1], cache[1, :LAT, :])
     pack(0)
-    partials0 = start(partial_copies(0))
+    partials0 = partial_copies(0)
 
     arrived(others1 + forward_z1 + forward_x1)
     assemble(1)

time: 48.1 us -> 48.1 us (level)
  no operation moved by 1% of the time
where the time goes in v7:
time: 48.1 us; the launch traced here: 48 us
  Pallas kernels  46.6 us (97%)
  local copies, waits for them, and re-layouts  1.35 us (3%)
    pallas_call x1, Pallas kernels, body(): pl.pallas_call(kernel, out_shape=jax.ShapeDtypeStruct((rows, 128), BF16),...  46.6 us
    unnamed x1, local copies, waits for them, and re-layouts  1.35 us

profile of v7, /device:TPU:0, one launch (start us, length us, event | category | flops | bytes accessed | tf_op | source)
XLA Modules:
  0.0 48.0 jit_solution(7828609299874506476)
XLA Ops:
  0.0 46.6 %latent_attention.1 = bf16[96,128]{1,0:T(8,128)(2,1)} custom-call(bf16[96,128]{1,0:T(8,128)(2,1)} %bitcast.9, bf16[96,64]{1,0:T(8,128)(2,1)} %bitcast.10, bf16[8,128,512]{2,1,0:T(8,128)(2,1)} %wa_hbm.1, bf16[8,512,128]{2,1,0:T(8,128)(2,1)} %wv_hbm.1, bf16[2,576,2048]{2,1,0:T(8,128)(2,1)} %bitcast.6, s32[2]{0:T(128)} %len_hbm.1, ...), custom_call_target="tpu_custom_call" | custom-call | tf_op jit(solution)/shard_map/latent_attention/pallas_call | solution.py:497
  46.6 1.3 %copy.11 = bf16[4,3,8,128]{3,2,1,0:T(8,128)(2,1)} copy(bf16[4,3,8,128]{3,2,1,0:T(8,128)(2,1)} %bitcast.8) | data formatting | bytes 49152
